TPU v7x, 512 devices: a whole 4x8x8 slice. The times are simulated.
512 devices in a mesh: dom: 128 (over y, z, core), feat: 4 (over x).
Axes of the slice: x: 4, y: 8, z: 8, core: 2. Of those that a mesh axis runs over, the one named last changes fastest.
Arguments:
- features: bfloat16 [32768, 768], P('dom', 'feat'), may hold values from -6 to 6
- pre_act: bfloat16 [32768, 256], P('dom'), may hold values from -6 to 6
- out_grad: bfloat16 [32768, 256], P('dom', 'feat'), may hold values from -0.03125 to 0.03125
- w_second: bfloat16 [256, 256], P(None, 'feat'), may hold values from -0.375 to 0.375
- adj_tiles: int32 [256, 6, 128, 128], P('dom'), may hold values from 0 to 3, as said below
- tile_cols: int32 [256, 6], P('dom'), may hold values from 0 to 3, as said below
- tile_live: int32 [256], P('dom'), may hold values from 1 to 6, as said below
- halo_counts: int32 [16384], P('dom'), may hold values from 0 to 2, as said below
- border_rows: int32 [16384, 2], P('dom'), may hold values from 0 to 255
Outputs:
- grad_first: float32 [768, 256], P('feat')
- grad_second: float32 [256, 256], P(None, 'feat')
Inputs may be any that keep to these rules, and one draw needn't show every extreme that they name: `adj_tiles`: entries are edge counts; every diagonal entry of slot 0 is at least 1. `tile_cols`: column blocks count the 2 own blocks first, then the boundary slots; slot 0 of a partition's row block b is its own block b. `tile_live`: every partition has a row block with all 6 slots live. `halo_counts`: entry p * 128 + p is 0; every partition keeps exactly 2 live slots for some peer.
All inputs are finite; a program needn't handle non-finite values.
Results may differ from a plain program's by a relative error of at most 0.0085.
Values may be sent and summed in bfloat16 or wider, within the bound.
A program may use at most 64 MiB of HBM per device.

v0:
```python
import jax
import jax.numpy as jnp
from jax import lax
from jax.sharding import PartitionSpec as P


def three_parts(values):
    high = values.astype(jnp.bfloat16)
    rest = values - high.astype(jnp.float32)
    middle = rest.astype(jnp.bfloat16)
    lowest = (rest - middle.astype(jnp.float32)).astype(jnp.bfloat16)
    return jnp.concatenate([high, middle, lowest], axis=-1)


def fold_last(values, span):
    return values[..., :span] + values[..., span : 2 * span] + values[..., 2 * span :]


def spread_forward(tile_set, col_ids, extended, tile_edge):
    columns = extended.shape[1]
    blocks = extended.reshape(-1, tile_edge, columns)
    summed = jnp.einsum(
        "bsij,bsjw->biw", tile_set, blocks[col_ids], preferred_element_type=jnp.float32
    )
    return summed.reshape(-1, columns)


def spread_back(tile_set, col_ids, source, tile_edge, col_blocks, split_terms):
    columns = source.shape[1]
    if split_terms:
        pieces = three_parts(source)
        blocks = pieces.reshape(-1, tile_edge, 3 * columns)
        products = fold_last(
            jnp.einsum("bsij,biw->bsjw", tile_set, blocks, preferred_element_type=jnp.float32),
            columns,
        )
    else:
        blocks = source.reshape(-1, tile_edge, columns)
        products = jnp.einsum(
            "bsij,biw->bsjw", tile_set, blocks, preferred_element_type=jnp.float32
        )
    one_hot = (col_ids[:, :, None] == jnp.arange(col_blocks)[None, None, :]).astype(jnp.float32)
    placed = jnp.einsum("bsc,bsjw->cjw", one_hot, products, precision=lax.Precision.HIGHEST)
    return placed.reshape(col_blocks * tile_edge, columns)


def body(
    features, pre_act, out_grad, w_second, adj_tiles, tile_cols, tile_live, halo_counts, border_rows
):
    tile_edge = adj_tiles.shape[2]
    slot_count = adj_tiles.shape[1]
    local_rows = pre_act.shape[0]
    hidden = pre_act.shape[1]
    peer_count = lax.axis_size("dom")
    per_peer = border_rows.shape[1]
    halo_rows = peer_count * per_peer
    col_blocks = (local_rows + halo_rows) // tile_edge
    halo_flags = (jnp.arange(per_peer)[None, :] < halo_counts[:, None]).reshape(halo_rows)
    column_live = jnp.concatenate([jnp.ones((local_rows,), jnp.bool_), halo_flags]).reshape(
        col_blocks, tile_edge
    )
    slot_flags = jnp.arange(slot_count)[None, :] < tile_live[:, None]
    kept_mask = column_live[tile_cols] & slot_flags[:, :, None]
    tile_set = jnp.where(kept_mask[:, :, None, :], adj_tiles, 0).astype(jnp.bfloat16)
    degree = jnp.sum(tile_set, axis=(1, 3), dtype=jnp.float32).reshape(local_rows, 1)
    activated = jnp.maximum(pre_act, 0)
    outgoing = activated[border_rows]
    arrived = lax.all_to_all(outgoing, "dom", split_axis=0, concat_axis=0, tiled=True)
    extended = jnp.concatenate([activated, arrived.reshape(halo_rows, hidden)], axis=0)
    mixed_act = (spread_forward(tile_set, tile_cols, extended, tile_edge) / degree).astype(
        jnp.bfloat16
    )
    second_part = lax.dot_general(
        mixed_act, out_grad, (((0,), (0,)), ((), ())), preferred_element_type=jnp.float32
    )
    grad_second = lax.psum(second_part, "dom")
    partial_rows = lax.dot_general(
        out_grad, w_second, (((1,), (1,)), ((), ())), preferred_element_type=jnp.float32
    )
    back_rows = lax.psum(partial_rows, "feat")
    scaled_rows = (back_rows / degree).astype(jnp.bfloat16)
    spread = spread_back(tile_set, tile_cols, scaled_rows, tile_edge, col_blocks, False)
    returned = lax.all_to_all(
        spread[local_rows:].reshape(peer_count, per_peer, hidden),
        "dom",
        split_axis=0,
        concat_axis=0,
        tiled=True,
    )
    grad_act = (
        spread[:local_rows].at[border_rows.reshape(-1)].add(returned.reshape(halo_rows, hidden))
    )
    grad_pre = jnp.where(pre_act > 0, grad_act, 0.0).astype(jnp.bfloat16)
    weighted = grad_pre.astype(jnp.float32) / degree
    carried = spread_back(tile_set, tile_cols, weighted, tile_edge, col_blocks, True)
    sent_back = lax.all_to_all(
        carried[local_rows:].reshape(peer_count, per_peer, hidden).astype(jnp.bfloat16),
        "dom",
        split_axis=0,
        concat_axis=0,
        tiled=True,
    ).astype(jnp.float32)
    gathered_grad = (
        carried[:local_rows].at[border_rows.reshape(-1)].add(sent_back.reshape(halo_rows, hidden))
    )
    stacked = lax.dot_general(
        features,
        three_parts(gathered_grad),
        (((0,), (0,)), ((), ())),
        preferred_element_type=jnp.float32,
    )
    first_part = fold_last(stacked, hidden)
    grad_first = lax.psum(first_part, "dom")
    return (grad_first, grad_second)


def solution(mesh):
    in_specs = (
        P("dom", "feat"),
        P("dom", None),
        P("dom", "feat"),
        P(None, "feat"),
        P("dom", None, None, None),
        P("dom", None),
        P("dom"),
        P("dom"),
        P("dom", None),
    )
    out_specs = (P("feat", None), P(None, "feat"))
    return jax.shard_map(body, mesh=mesh, in_specs=in_specs, out_specs=out_specs, check_vma=False)
```

profile of v0, /device:TPU:1, one launch (start us, length us, event | category | flops | bytes accessed | tf_op | source)
XLA Modules:
  0.0 339.3 jit_solution(2366662642721510288)
XLA Ops:
  7.3 0.8 compare_select_fusion.1
  8.0 0.1 copy.21
  8.1 0.1 reshape.131
  8.3 0.9 broadcast_maximum_fusion
  9.2 1.2 gather_fusion.1
  10.4 0.7 reshape.130
  11.1 18.4 %all-to-all-start.2 = ((bf16[128,2,256]{2,1,0:T(2,128)(2,1)}), bf16[128,2,256]{2,1,0:T(2,128)(2,1)S(1)}, u32[]{:S(2)}, u32[]{:S(2)}) async-start(bf16[128,2,256]{2,1,0:T(2,128)(2,1)} %reshape.130), calls=%async_computation.2 | async-start | bytes 262144 | tf_op jit(solution)/shard_map/all_to_all | solution.py:68
  29.5 0.0 all-reduce.5.cloned.1.call-start
  29.6 0.9 fusion.27
  30.5 0.1 iota_compare_fusion.2
  30.6 0.1 reshape.123
  30.7 0.1 iota_compare_fusion
  30.8 0.1 lt.58
  30.9 0.6 gather_fusion
  31.5 0.1 broadcast_and_fusion
  31.6 0.1 copy.15
  31.7 0.1 reshape.110
  31.9 0.2 convert_reduce_fusion
  32.1 51.7 %all-reduce.5.cloned.1.call-done = f32[256,256]{1,0:T(8,128)} async-done(((f32[256,256]{1,0:T(8,128)}), f32[256,256]{1,0:T(8,128)}) %all-reduce.5.cloned.1.call-update) | async-done | bytes 262160 | tf_op jit(solution)/shard_map/psum | solution.py:80
  83.7 1.1 divide_convert_fusion
  84.8 0.4 fusion.28
  85.2 2.3 fusion.7
  87.5 0.2 fusion.25
  87.8 0.8 reshape.111
  88.6 16.4 %all-to-all-start = ((f32[128,2,256]{2,1,0:T(2,128)}), f32[128,2,256]{2,1,0:T(2,128)S(1)}, u32[]{:S(2)}, u32[]{:S(2)}) async-start(f32[128,2,256]{2,1,0:T(2,128)} %reshape.111), calls=%async_computation | async-start | bytes 524288 | tf_op jit(solution)/shard_map/all_to_all | solution.py:83
  105.0 0.1 reshape.116
  105.1 0.6 gather_fusion.2
  105.7 0.3 fusion.30
  106.0 13.2 %all-to-all-done = f32[128,2,256]{2,1,0:T(2,128)S(1)} async-done(((f32[128,2,256]{2,1,0:T(2,128)}), f32[128,2,256]{2,1,0:T(2,128)S(1)}, u32[]{:S(2)}, u32[]{:S(2)}) %all-to-all-start) | async-done | bytes 262176 | tf_op jit(solution)/shard_map/all_to_all | solution.py:83
  119.2 0.2 reshape.149
  119.4 2.3 scatter_fusion
  121.7 0.1 fusion.24
  121.9 0.8 fusion.29
  122.8 0.3 slice_add_fusion
  123.1 2.3 fusion.4
  125.4 0.1 slice.78
  125.5 0.7 convert_element_type.65
  126.3 7.0 %all-to-all-start.1 = ((bf16[128,2,256]{2,1,0:T(2,128)(2,1)}), bf16[128,2,256]{2,1,0:T(2,128)(2,1)S(1)}, u32[]{:S(2)}, u32[]{:S(2)}) async-start(bf16[128,2,256]{2,1,0:T(2,128)(2,1)} %convert_element_type.65), calls=%async_computation.1 | async-start | bytes 262144 | tf_op jit(solution)/shard_map/all_to_all | solution.py:96
  133.2 0.0 all-reduce.7.cloned.1.call-start
  133.3 0.1 slice.62
  133.4 0.8 fusion.31
  134.2 11.3 %all-to-all-done.1 = bf16[128,2,256]{2,1,0:T(2,128)(2,1)S(1)} async-done(((bf16[128,2,256]{2,1,0:T(2,128)(2,1)}), bf16[128,2,256]{2,1,0:T(2,128)(2,1)S(1)}, u32[]{:S(2)}, u32[]{:S(2)}) %all-to-all-start.1) | async-done | bytes 131104 | tf_op jit(solution)/shard_map/all_to_all | solution.py:96
  145.6 2.1 scatter_fusion.1
  147.7 0.2 convolution_bitcast_fusion
  148.0 0.7 slice_add_fusion.2
  148.7 180.6 %all-reduce.7.cloned.1.call-done = (f32[192,256]{1,0:T(8,128)}, f32[256,64]{0,1:T(8,128)}) async-done(((f32[192,256]{1,0:T(8,128)}, f32[256,64]{0,1:T(8,128)}), (f32[192,256]{1,0:T(8,128)}, f32[256,64]{0,1:T(8,128)})) %all-reduce.7.cloned.1.call-update) | async-done | bytes 262160 | tf_op jit(solution)/shard_map/psum | solution.py:113
  329.3 1.6 copy.42
  331.0 1.5 copy.43
  (36 shorter events, 0.4 us)
Async XLA Ops:
  7.2 140.5 %copy-start = (bf16[256,192]{0,1:T(8,128)(2,1)S(1)}, bf16[256,192]{0,1:T(8,128)(2,1)}, u32[]{:S(2)}) copy-start(bf16[256,192]{0,1:T(8,128)(2,1)} %param.9) | copy-start | bytes 294916
  7.2 24.4 %copy-start.6 = (s32[128,2]{0,1:T(2,128)S(1)}, s32[128,2]{0,1:T(2,128)}, u32[]{:S(2)}) copy-start(s32[128,2]{0,1:T(2,128)} %param.17) | copy-start | bytes 3076
  7.2 22.4 %copy-start.3 = (bf16[256,64]{0,1:T(8,128)(2,1)S(1)}, bf16[256,64]{0,1:T(8,128)(2,1)}, u32[]{:S(2)}) copy-start(bf16[256,64]{0,1:T(8,128)(2,1)} %param.11) | copy-start | bytes 98308
  7.2 22.4 %copy-start.4 = (bf16[256,64]{0,1:T(8,128)(2,1)S(1)}, bf16[256,64]{0,1:T(8,128)(2,1)}, u32[]{:S(2)}) copy-start(bf16[256,64]{0,1:T(8,128)(2,1)} %param.12) | copy-start | bytes 98308
  7.2 23.3 %copy-start.8 = (s32[2]{0:T(128)S(1)}, s32[2]{0:T(128)}, u32[]{:S(2)}) copy-start(s32[2]{0:T(128)} %param.15) | copy-start | bytes 28
  7.2 23.4 %copy-start.5 = (s32[2,6]{1,0:T(2,128)S(1)}, s32[2,6]{1,0:T(2,128)}, u32[]{:S(2)}) copy-start(s32[2,6]{1,0:T(2,128)} %param.14) | copy-start | bytes 148
  7.2 23.5 %copy-start.7 = (s32[128]{0:T(128)S(1)}, s32[128]{0:T(128)}, u32[]{:S(2)}) copy-start(s32[128]{0:T(128)} %param.16) | copy-start | bytes 1540
  7.2 24.6 %copy-start.1 = (s32[2,6,128,128]{3,2,1,0:T(8,128)S(1)}, s32[2,6,128,128]{3,2,1,0:T(8,128)}, u32[]{:S(2)}) copy-start(s32[2,6,128,128]{3,2,1,0:T(8,128)} %param.13) | copy-start | bytes 2359300
  11.1 77.5 %all-to-all-start.2 = ((bf16[128,2,256]{2,1,0:T(2,128)(2,1)}), bf16[128,2,256]{2,1,0:T(2,128)(2,1)S(1)}, u32[]{:S(2)}, u32[]{:S(2)}) async-start(bf16[128,2,256]{2,1,0:T(2,128)(2,1)} %reshape.130), calls=%async_computation.2 | async-start | bytes 262144 | tf_op jit(solution)/shard_map/all_to_all | solution.py:68
  29.5 54.2 %all-reduce.5.cloned.1.call-start = ((), (), s32[]{:S(2)}) async-start(), calls=%async_computation.3 | async-start | bytes 524288 | tf_op jit(solution)/shard_map/psum | solution.py:80
  88.6 30.6 %all-to-all-start = ((f32[128,2,256]{2,1,0:T(2,128)}), f32[128,2,256]{2,1,0:T(2,128)S(1)}, u32[]{:S(2)}, u32[]{:S(2)}) async-start(f32[128,2,256]{2,1,0:T(2,128)} %reshape.111), calls=%async_computation | async-start | bytes 524288 | tf_op jit(solution)/shard_map/all_to_all | solution.py:83
  119.4 2.3 copy-start.2
  126.3 19.3 %all-to-all-start.1 = ((bf16[128,2,256]{2,1,0:T(2,128)(2,1)}), bf16[128,2,256]{2,1,0:T(2,128)(2,1)S(1)}, u32[]{:S(2)}, u32[]{:S(2)}) async-start(bf16[128,2,256]{2,1,0:T(2,128)(2,1)} %convert_element_type.65), calls=%async_computation.1 | async-start | bytes 262144 | tf_op jit(solution)/shard_map/all_to_all | solution.py:96
  133.2 196.1 %all-reduce.7.cloned.1.call-start = ((), (), s32[]{:S(2)}) async-start(), calls=%async_computation.4 | async-start | bytes 524288 | tf_op jit(solution)/shard_map/psum | solution.py:113
Sparse Core Ops, SparseCore 0:
  32.7 51.0 all-reduce.4
  148.8 180.4 all-reduce.6
where the time goes:
time: 341 us; the launch traced here: 339 us
  waiting for transfers between devices  257 us (75%)
  starting transfers between devices  41.9 us (12%)
  between operations  14.4 us (4%)
  local copies, waits for them, and re-layouts  9.26 us (3%)
  other arithmetic  8.79 us (3%)
  matrix products  8.03 us (2%)
    psum x1, waiting for transfers between devices, body(): grad_first = lax.psum(first_part, 'dom')  181 us
    psum x1, waiting for transfers between devices, body(): back_rows = lax.psum(partial_rows, 'feat')  51.7 us
    all_to_all x1, starting transfers between devices, body(): lax.all_to_all(outgoing, 'dom', split_axis=0, concat_axis=0, tiled=True)  18.4 us
    all_to_all x1, starting transfers between devices, body(): lax.all_to_all(spread[local_rows:].reshape(peer_count, per_peer, hidden),...  16.4 us
    all_to_all x1, waiting for transfers between devices, body(): lax.all_to_all(spread[local_rows:].reshape(peer_count, per_peer, hidden),...  13.2 us
    all_to_all x1, waiting for transfers between devices, body(): lax.all_to_all(carried[local_rows:].reshape(peer_count, per_peer, hidden)...  11.3 us
    all_to_all x1, starting transfers between devices, body(): lax.all_to_all(carried[local_rows:].reshape(peer_count, per_peer, hidden)...  6.96 us
  transfers between devices with their start and end apart: 5, of which 4 were waited for; matrix products, arithmetic and copies ran while one was open for 3% of the time, Pallas kernels for 0%

commit v1 on v0

v1 whole, which is shorter than its diff:
```python
import jax
import jax.numpy as jnp
from jax import lax
from jax.experimental import pallas as pl
from jax.experimental.pallas import tpu as pltpu
from jax.sharding import PartitionSpec as P

MESH = pl.DeviceIdType.MESH
BF16 = jnp.bfloat16
F32 = jnp.float32

NY = 8
NZC = 16
NZ = 8
NX = 4
PHASES = 12


def dot(a, b):
    return lax.dot_general(a, b, (((1,), (0,)), ((), ())), preferred_element_type=F32)


def dot_nt(a, b):
    return lax.dot_general(a, b, (((1,), (1,)), ((), ())), preferred_element_type=F32)


def rows_of(ref, start, size):
    return ref.at[pl.ds(pl.multiple_of(start, size), size)]


def kernel(
    ft_hbm, pa_hbm, gt_hbm, wt_hbm, adj_hbm, cols_ref, live_ref, hc_hbm, br_hbm,
    o1_ref, o2_ref,
    ft, pa, gt, wt, adj, hc, br,
    amat, s0, r0, t0, u0, s1, r1, t1, u1, wall, sall,
    q0s, q1s, q0, q1, w0, w1, v0, v1, f0, f1,
    load_sem, send_sem, recv_sem,
):
    dom = lax.axis_index("dom")
    feat = lax.axis_index("feat")
    y = dom // NZC
    zc = dom % NZC
    z = zc // 2
    core = dom % 2
    yc = y * 2 + core

    def dom_y(k):
        return ((y + k) % NY) * NZC + zc

    def dom_zc(k):
        return y * NZC + (zc + k) % NZC

    def dom_z(k):
        return y * NZC + ((z + k) % NZ) * 2 + core

    def dom_yc(k):
        other = (yc + k) % 16
        return (other // 2) * NZC + z * 2 + other % 2

    loads = []
    for i, (src, dst) in enumerate(
        [(br_hbm, br), (adj_hbm, adj), (ft_hbm, ft), (hc_hbm, hc), (gt_hbm, gt), (wt_hbm, wt), (pa_hbm, pa)]
    ):
        copy = pltpu.make_async_copy(src, dst, load_sem.at[i])
        copy.start()
        loads.append(copy)
    ld_br, ld_adj, ld_ft, ld_hc, ld_gt, ld_wt, ld_pa = loads

    barrier = pltpu.get_barrier_semaphore()

    def greet(d, f):
        pl.semaphore_signal(barrier, inc=1, device_id=(d, f), device_id_type=MESH)

    for k in range(1, NY):
        greet(dom_y(k), feat)
    for k in range(1, NZC):
        greet(dom_zc(k), feat)
    for k in range(1, NY):
        greet(((y + k) % NY) * NZC + z * 2 + (1 - core), feat)
    for k in range(1, NX):
        greet(dom, (feat + k) % NX)
    partners = (NY - 1) * 2 + (NZC - 1) + (NX - 1)

    def send(phase, k, src, dst, device):
        copy = pltpu.make_async_remote_copy(
            src_ref=src,
            dst_ref=dst,
            send_sem=send_sem.at[phase, k],
            recv_sem=recv_sem.at[phase, k],
            device_id=device,
            device_id_type=MESH,
        )
        copy.start()
        return copy

    def scatter_y(phase, src, dst, rows):
        copies = []
        for k in range(1, NY):
            copies.append(
                send(phase, k, rows_of(src, ((y + k) % NY) * rows, rows), rows_of(dst, y * rows, rows), (dom_y(k), feat))
            )
        rows_of(dst, y * rows, rows)[...] = rows_of(src, y * rows, rows)[...]
        return copies

    def scatter_zc(phase, src, dst, rows):
        copies = []
        for k in range(1, NZC):
            copies.append(
                send(phase, k, rows_of(src, ((zc + k) % NZC) * rows, rows), rows_of(dst, zc * rows, rows), (dom_zc(k), feat))
            )
        rows_of(dst, zc * rows, rows)[...] = rows_of(src, zc * rows, rows)[...]
        return copies

    def arrive(copies):
        for copy in copies:
            copy.wait_recv()

    n = 256
    rows_i = lax.broadcasted_iota(jnp.int32, (n, n), 0)
    lanes_i = lax.broadcasted_iota(jnp.int32, (n, n), 1)
    one_hot = lambda cond: jnp.where(cond, 1.0, 0.0).astype(BF16)
    eye = one_hot(rows_i == lanes_i)
    perm = one_hot(lanes_i == ((rows_i >> 1) & 7) * 32 + (rows_i >> 4) * 2 + (rows_i & 1))
    perm_t = one_hot(lanes_i == ((rows_i >> 1) & 15) * 16 + (rows_i >> 5) * 2 + (rows_i & 1))
    eye128 = one_hot(
        lax.broadcasted_iota(jnp.int32, (128, 128), 0) == lax.broadcasted_iota(jnp.int32, (128, 128), 1)
    )
    peer_i = lax.broadcasted_iota(jnp.int32, (128, n), 0)
    slot_i = lax.broadcasted_iota(jnp.int32, (128, n), 1)
    even = one_hot(slot_i == 2 * peer_i)
    odd = one_hot(slot_i == 2 * peer_i + 1)

    ld_br.wait()
    border = br[...].astype(F32).astype(BF16)
    slot_row = dot(jnp.broadcast_to(border[0:1], (16, 128)), even) + dot(
        jnp.broadcast_to(border[1:2], (16, 128)), odd
    )
    hot_t = one_hot(rows_i.astype(F32) == slot_row[0:1])
    hot = dot_nt(eye, hot_t).astype(BF16)
    hot_p = dot_nt(perm, hot_t).astype(BF16)

    ld_ft.wait()
    s0[...] = dot_nt(hot, ft[0:128]).astype(BF16)

    pl.semaphore_wait(barrier, partners)
    c_s0 = scatter_y(0, s0, r0, 32)
    ld_wt.wait()
    c_w = []
    for k in range(1, NX):
        c_w.append(send(4, k, wt, rows_of(wall, feat * 64, 64), (dom, (feat + k) % NX)))
    rows_of(wall, feat * 64, 64)[...] = wt[...]

    ld_hc.wait()
    counts = jnp.broadcast_to(hc[...].astype(F32).astype(BF16), (16, 128))
    slot_counts = dot(counts, even + odd)[0:1]
    parity = (lax.broadcasted_iota(jnp.int32, (1, n), 1) & 1).astype(F32)
    flags = jnp.where(parity < slot_counts, 1.0, 0.0)
    ld_adj.wait()
    for b in range(2):
        for cb in range(4):
            total = jnp.zeros((128, 128), jnp.int32)
            for s in range(6):
                keep = jnp.logical_and(cols_ref[b, s] == cb, s < live_ref[b])
                total = total + (adj[b, s] & jnp.where(keep, -1, 0))
            total = total.astype(F32)
            if cb >= 2:
                total = total * flags[:, (cb - 2) * 128 : (cb - 1) * 128]
            amat[b * 128 : (b + 1) * 128, cb * 128 : (cb + 1) * 128] = total.astype(BF16)
    degree = dot_nt(jnp.ones((16, 512), BF16), amat[...])[0:1]

    ld_gt.wait()
    scaled = gt[...].astype(F32) / degree
    high = scaled.astype(BF16)
    low = (scaled - high.astype(F32)).astype(BF16)
    spread = dot(jnp.concatenate([high, low], axis=0), amat[...])
    spread = spread[0:64] + spread[64:128]
    own_part = spread[:, 0:256]
    zeros64 = jnp.zeros((64, n), BF16)
    s1[...] = (
        dot_nt(hot_p, jnp.concatenate([ft[128:192], zeros64], axis=0))
        + dot_nt(perm, jnp.concatenate([zeros64, spread[:, 256:512].astype(BF16)], axis=0))
    ).astype(BF16)
    c_s1 = scatter_zc(2, s1, r1, 16)

    a_own = amat[:, 0:256]
    a_halo = amat[:, 256:512]

    arrive(c_s0)
    t0[...] = dot(perm, r0[...]).astype(BF16)
    c_u0 = scatter_zc(1, t0, u0, 16)

    a_halo_p = dot_nt(a_halo, perm).astype(BF16)
    mixed = dot_nt(ft[...], a_own)

    arrive(c_s1)
    t1[...] = dot(perm_t, r1[...]).astype(BF16)
    c_u1 = scatter_y(3, t1, u1, 32)

    ld_pa.wait()
    pre = pa[...].astype(F32)
    act = jnp.maximum(pre, 0.0).astype(BF16)
    mask_t = dot_nt(eye, one_hot(pre > 0.0))
    arrive(c_w)
    w_full = dot_nt(eye, wall[...]).astype(BF16)

    arrive(c_u1)
    x1 = dot_nt(eye128, u1[...]).astype(BF16)
    gathered = (own_part + dot(x1[64:128], hot)).astype(BF16)
    rows_of(sall, feat * 64, 64)[...] = gathered
    c_x = []
    for k in range(1, NX):
        c_x.append(
            send(5, k, rows_of(sall, feat * 64, 64), rows_of(sall, feat * 64, 64), (dom, (feat + k) % NX))
        )
    second = dot(gathered, act)

    arrive(c_u0)
    x0 = dot_nt(eye128, u0[...]).astype(BF16)
    mixed_low = (mixed[0:128] + dot_nt(x0, a_halo_p)) / degree
    mixed_top = (mixed[128:192] + dot_nt(x1[0:64], a_halo)) / degree
    mixed_in = jnp.concatenate([mixed_low.astype(BF16), mixed_top.astype(BF16)], axis=0)

    arrive(c_x)
    grad_act = dot(w_full, sall[...])
    grad_pre = jnp.where(mask_t > 0.5, grad_act, 0.0).astype(BF16)
    first = dot_nt(mixed_in, grad_pre)

    q0s[0:192] = first[:, 0:128].astype(BF16)
    q1s[0:192] = first[:, 128:256].astype(BF16)
    q0s[192:256] = second[:, 0:128].astype(BF16)
    q1s[192:256] = second[:, 128:256].astype(BF16)

    c_q0, c_q1 = [], []
    for k in range(1, 16):
        c_q0.append(
            send(6, k, rows_of(q0s, ((yc + k) % 16) * 16, 16), rows_of(q0, yc * 16, 16), (dom_yc(k), feat))
        )
        c_q1.append(
            send(7, k, rows_of(q1s, ((zc + k) % 16) * 16, 16), rows_of(q1, zc * 16, 16), (dom_zc(k), feat))
        )
    rows_of(q0, yc * 16, 16)[...] = rows_of(q0s, yc * 16, 16)[...]
    rows_of(q1, zc * 16, 16)[...] = rows_of(q1s, zc * 16, 16)[...]

    def total_of(ref, members):
        total = ref[0:16].astype(F32)
        for i in range(1, members):
            total = total + ref[i * 16 : (i + 1) * 16].astype(F32)
        return total.astype(BF16)

    arrive(c_q0)
    part0 = total_of(q0, 16)
    w0[...] = part0
    c_v0 = []
    for k in range(1, NZ):
        c_v0.append(send(8, k, w0, rows_of(v0, z * 16, 16), (dom_z(k), feat)))
    rows_of(v0, z * 16, 16)[...] = part0
    arrive(c_q1)
    part1 = total_of(q1, 16)
    w1[...] = part1
    c_v1 = []
    for k in range(1, NY):
        c_v1.append(send(9, k, w1, rows_of(v1, y * 16, 16), (dom_y(k), feat)))
    rows_of(v1, y * 16, 16)[...] = part1

    arrive(c_v0)
    rows_of(f0, yc * 16, 16)[...] = total_of(v0, 8)
    c_f0 = []
    for k in range(1, 16):
        c_f0.append(
            send(10, k, rows_of(f0, yc * 16, 16), rows_of(f0, yc * 16, 16), (dom_yc(k), feat))
        )
    arrive(c_v1)
    rows_of(f1, zc * 16, 16)[...] = total_of(v1, 8)
    c_f1 = []
    for k in range(1, 16):
        c_f1.append(
            send(11, k, rows_of(f1, zc * 16, 16), rows_of(f1, zc * 16, 16), (dom_zc(k), feat))
        )
    arrive(c_f0)
    o1_ref[:, 0:128] = f0[0:192].astype(F32)
    o2_ref[:, 0:128] = f0[192:256].astype(F32)
    arrive(c_f1)
    o1_ref[:, 128:256] = f1[0:192].astype(F32)
    o2_ref[:, 128:256] = f1[192:256].astype(F32)

    for copies in (c_s0, c_w, c_s1, c_u0, c_u1, c_x, c_q0, c_q1, c_v0, c_v1, c_f0, c_f1):
        for copy in copies:
            copy.wait_send()


def body(
    features, pre_act, out_grad, w_second, adj_tiles, tile_cols, tile_live, halo_counts, border_rows
):
    anywhere = pl.BlockSpec(memory_space=pl.ANY)
    smem = pl.BlockSpec(memory_space=pltpu.SMEM)
    vmem = pl.BlockSpec(memory_space=pltpu.VMEM)
    half = pltpu.VMEM((256, 128), BF16)
    square = pltpu.VMEM((256, 256), BF16)
    grad_first, grad_second_t = pl.pallas_call(
        kernel,
        out_shape=(
            jax.ShapeDtypeStruct((192, 256), F32),
            jax.ShapeDtypeStruct((64, 256), F32),
        ),
        in_specs=[anywhere, anywhere, anywhere, anywhere, anywhere, smem, smem, anywhere, anywhere],
        out_specs=(vmem, vmem),
        scratch_shapes=[
            pltpu.VMEM((192, 256), BF16),
            square,
            pltpu.VMEM((64, 256), BF16),
            pltpu.VMEM((64, 256), BF16),
            pltpu.VMEM((2, 6, 128, 128), jnp.int32),
            pltpu.VMEM((1, 128), jnp.int32),
            pltpu.VMEM((2, 128), jnp.int32),
            pltpu.VMEM((256, 512), BF16),
            half, half, half, half, half, half, half, half,
            square, square,
            half, half, half, half,
            pltpu.VMEM((16, 128), BF16),
            pltpu.VMEM((16, 128), BF16),
            pltpu.VMEM((128, 128), BF16),
            pltpu.VMEM((128, 128), BF16),
            half, half,
            pltpu.SemaphoreType.DMA((7,)),
            pltpu.SemaphoreType.DMA((PHASES, 16)),
            pltpu.SemaphoreType.DMA((PHASES, 16)),
        ],
        compiler_params=pltpu.CompilerParams(collective_id=0, has_side_effects=True),
        name="sage_backward",
    )(
        features.T, pre_act, out_grad.T, w_second.T, adj_tiles, tile_cols, tile_live,
        halo_counts.reshape(1, 128), border_rows.T,
    )
    return grad_first, grad_second_t.T


def solution(mesh):
    in_specs = (
        P("dom", "feat"),
        P("dom", None),
        P("dom", "feat"),
        P(None, "feat"),
        P("dom", None, None, None),
        P("dom", None),
        P("dom"),
        P("dom"),
        P("dom", None),
    )
    out_specs = (P("feat", None), P(None, "feat"))
    return jax.shard_map(body, mesh=mesh, in_specs=in_specs, out_specs=out_specs, check_vma=False)
```

time: 341 us -> 55.1 us (0.16)
  waiting for transfers between devices: 257 us -> 0 us
  Pallas kernels: 0 us -> 52 us
  starting transfers between devices: 41.9 us -> 0 us
  between operations: 14.4 us -> 0.65 us
  other arithmetic: 8.79 us -> 0 us
  matrix products: 8.03 us -> 0 us
  local copies, waits for them, and re-layouts: 9.26 us -> 2.28 us
    psum x2 -> x0, waiting for transfers between devices: 232 us -> none  [the longest x1 181 us: body(): grad_first = lax.psum(first_part, 'dom')]
    pallas_call x0 -> x1, Pallas kernels: none -> 52 us  [body(): pl.pallas_call(kernel, out_shape=(jax.ShapeDtypeStruct((192, 256), F32),...]
    all_to_all x3 -> x0, starting transfers between devices: 41.8 us -> none  [the longest x1 18.4 us: body(): lax.all_to_all(outgoing, 'dom', split_axis=0, concat_axis=0, tiled=True)]
    all_to_all x3 -> x0, waiting for transfers between devices: 24.6 us -> none  [the longest x1 13.2 us: body(): lax.all_to_all(spread[local_rows:].reshape(peer_count, per_peer, hidden),...]
    dot_general x8 -> x0, matrix products: 8.03 us -> none  [the longest x2 4.59 us: spread_back(): jnp.einsum('bsc,bsjw->cjw', one_hot, products, precision=lax.Precision.HI...]
    scatter-add x2 -> x0, other arithmetic: 4.34 us -> none  [the longest x1 2.26 us: body(): spread[:local_rows].at[border_rows.reshape(-1)]]
  transfers between devices with their start and end apart: 5 -> 0, of which waited for: 4 -> 0; matrix products, arithmetic and copies ran while one was open for 3% -> 0% of each run, Pallas kernels for 0% -> 0%
where the time goes in v1:
time: 55.1 us; the launch traced here: 55 us
  Pallas kernels  52 us (94%)
  local copies, waits for them, and re-layouts  2.28 us (4%)
  between operations  0.65 us (1%)
    pallas_call x1, Pallas kernels, body(): pl.pallas_call(kernel, out_shape=(jax.ShapeDtypeStruct((192, 256), F32),...  52 us
    unnamed x4, local copies, waits for them, and re-layouts  2.28 us

profile of v1, /device:TPU:1, one launch (start us, length us, event | category | flops | bytes accessed | tf_op | source)
XLA Modules:
  0.0 55.0 jit_solution(16518160768990438425)
XLA Ops:
  0.6 52.0 %sage_backward.1 = (f32[192,256]{1,0:T(8,128)}, f32[64,256]{1,0:T(8,128)}) custom-call(bf16[192,256]{1,0:T(8,128)(2,1)} %bitcast.6, bf16[256,256]{1,0:T(8,128)(2,1)} %pa_hbm.1, bf16[64,256]{1,0:T(8,128)(2,1)} %bitcast.8, bf16[64,256]{1,0:T(8,128)(2,1)} %bitcast.9, s32[2,6,128,128]{3,2,1,0:T(8,128)} %adj_hbm.1, s32[2,6]{1,0:T(2,128)} %cols_ref.1, s32[2]{0:T(128)} %live_ref.1, ...), custom_call_target="tpu_custom_call" | custom-call | tf_op jit(solution)/shard_map/sage_backward/pallas_call | solution.py:299
  52.7 0.0 copy-start
  52.7 1.6 %copy.13 = f32[192,256]{1,0:T(8,128)} copy(f32[192,256]{1,0:T(8,128)} %get-tuple-element.8) | data formatting | bytes 393216
  54.3 0.0 copy-done
  54.3 0.6 %copy.14 = f32[256,64]{0,1:T(8,128)} copy(f32[256,64]{0,1:T(8,128)S(1)} %bitcast.7) | data formatting | bytes 131072
Async XLA Ops:
  52.7 1.7 %copy-start = (f32[64,256]{1,0:T(8,128)S(1)}, f32[64,256]{1,0:T(8,128)}, u32[]{:S(2)}) copy-start(f32[64,256]{1,0:T(8,128)} %get-tuple-element.5) | copy-start | bytes 196612

commit v2 on v1

--- a/solution.py
+++ b/solution.py
@@ -14,6 +14,9 @@
 NZ = 8
 NX = 4
 PHASES = 12
+FAR_8 = (4, 3, 5, 2, 6, 1, 7)
+FAR_16 = (8, 7, 9, 6, 10, 5, 11, 4, 12, 3, 13, 2, 14, 1, 15)
+FAR_4 = (2, 1, 3)
 
 
 def dot(a, b):
@@ -30,7 +33,7 @@
 
 def kernel(
     ft_hbm, pa_hbm, gt_hbm, wt_hbm, adj_hbm, cols_ref, live_ref, hc_hbm, br_hbm,
-    o1_ref, o2_ref,
+    out_ref,
     ft, pa, gt, wt, adj, hc, br,
     amat, s0, r0, t0, u0, s1, r1, t1, u1, wall, sall,
     q0s, q1s, q0, q1, w0, w1, v0, v1, f0, f1,
@@ -81,39 +84,43 @@
         greet(dom, (feat + k) % NX)
     partners = (NY - 1) * 2 + (NZC - 1) + (NX - 1)
 
-    def send(phase, k, src, dst, device):
+    def send(phase, src, dst, device):
         copy = pltpu.make_async_remote_copy(
             src_ref=src,
             dst_ref=dst,
-            send_sem=send_sem.at[phase, k],
-            recv_sem=recv_sem.at[phase, k],
+            send_sem=send_sem.at[phase],
+            recv_sem=recv_sem.at[phase],
             device_id=device,
             device_id_type=MESH,
         )
         copy.start()
-        return copy
 
     def scatter_y(phase, src, dst, rows):
-        copies = []
-        for k in range(1, NY):
-            copies.append(
-                send(phase, k, rows_of(src, ((y + k) % NY) * rows, rows), rows_of(dst, y * rows, rows), (dom_y(k), feat))
-            )
+        for k in FAR_8:
+            send(phase, rows_of(src, ((y + k) % NY) * rows, rows), rows_of(dst, y * rows, rows), (dom_y(k), feat))
         rows_of(dst, y * rows, rows)[...] = rows_of(src, y * rows, rows)[...]
-        return copies
 
     def scatter_zc(phase, src, dst, rows):
-        copies = []
-        for k in range(1, NZC):
-            copies.append(
-                send(phase, k, rows_of(src, ((zc + k) % NZC) * rows, rows), rows_of(dst, zc * rows, rows), (dom_zc(k), feat))
-            )
+        for k in FAR_16:
+            send(phase, rows_of(src, ((zc + k) % NZC) * rows, rows), rows_of(dst, zc * rows, rows), (dom_zc(k), feat))
         rows_of(dst, zc * rows, rows)[...] = rows_of(src, zc * rows, rows)[...]
-        return copies
-
-    def arrive(copies):
-        for copy in copies:
-            copy.wait_recv()
+
+    def all_of(phase, ref, rows):
+        return pltpu.make_async_remote_copy(
+            src_ref=ref.at[pl.ds(0, rows)],
+            dst_ref=ref.at[pl.ds(0, rows)],
+            send_sem=send_sem.at[phase],
+            recv_sem=recv_sem.at[phase],
+            device_id=(dom_y(1), feat),
+            device_id_type=MESH,
+        )
+
+    sent = []
+
+    def arrive(phase, ref, rows):
+        copies = all_of(phase, ref, rows)
+        copies.wait_recv()
+        sent.append(copies)
 
     n = 256
     rows_i = lax.broadcasted_iota(jnp.int32, (n, n), 0)
@@ -138,17 +145,6 @@
     hot_t = one_hot(rows_i.astype(F32) == slot_row[0:1])
     hot = dot_nt(eye, hot_t).astype(BF16)
     hot_p = dot_nt(perm, hot_t).astype(BF16)
-
-    ld_ft.wait()
-    s0[...] = dot_nt(hot, ft[0:128]).astype(BF16)
-
-    pl.semaphore_wait(barrier, partners)
-    c_s0 = scatter_y(0, s0, r0, 32)
-    ld_wt.wait()
-    c_w = []
-    for k in range(1, NX):
-        c_w.append(send(4, k, wt, rows_of(wall, feat * 64, 64), (dom, (feat + k) % NX)))
-    rows_of(wall, feat * 64, 64)[...] = wt[...]
 
     ld_hc.wait()
     counts = jnp.broadcast_to(hc[...].astype(F32).astype(BF16), (16, 128))
@@ -166,78 +162,76 @@
             if cb >= 2:
                 total = total * flags[:, (cb - 2) * 128 : (cb - 1) * 128]
             amat[b * 128 : (b + 1) * 128, cb * 128 : (cb + 1) * 128] = total.astype(BF16)
-    degree = dot_nt(jnp.ones((16, 512), BF16), amat[...])[0:1]
+    inverse = 1.0 / dot_nt(jnp.ones((16, 512), BF16), amat[...])[0:1]
 
     ld_gt.wait()
-    scaled = gt[...].astype(F32) / degree
+    scaled = gt[...].astype(F32) * inverse
     high = scaled.astype(BF16)
     low = (scaled - high.astype(F32)).astype(BF16)
     spread = dot(jnp.concatenate([high, low], axis=0), amat[...])
     spread = spread[0:64] + spread[64:128]
     own_part = spread[:, 0:256]
     zeros64 = jnp.zeros((64, n), BF16)
+    ld_ft.wait()
     s1[...] = (
         dot_nt(hot_p, jnp.concatenate([ft[128:192], zeros64], axis=0))
         + dot_nt(perm, jnp.concatenate([zeros64, spread[:, 256:512].astype(BF16)], axis=0))
     ).astype(BF16)
-    c_s1 = scatter_zc(2, s1, r1, 16)
+
+    pl.semaphore_wait(barrier, partners)
+    scatter_zc(2, s1, r1, 16)
+    s0[...] = dot_nt(hot, ft[0:128]).astype(BF16)
+    scatter_y(0, s0, r0, 32)
+    ld_wt.wait()
+    for k in FAR_4:
+        send(4, wt, rows_of(wall, feat * 64, 64), (dom, (feat + k) % NX))
+    rows_of(wall, feat * 64, 64)[...] = wt[...]
 
     a_own = amat[:, 0:256]
     a_halo = amat[:, 256:512]
-
-    arrive(c_s0)
-    t0[...] = dot(perm, r0[...]).astype(BF16)
-    c_u0 = scatter_zc(1, t0, u0, 16)
-
     a_halo_p = dot_nt(a_halo, perm).astype(BF16)
     mixed = dot_nt(ft[...], a_own)
-
-    arrive(c_s1)
-    t1[...] = dot(perm_t, r1[...]).astype(BF16)
-    c_u1 = scatter_y(3, t1, u1, 32)
-
     ld_pa.wait()
     pre = pa[...].astype(F32)
     act = jnp.maximum(pre, 0.0).astype(BF16)
     mask_t = dot_nt(eye, one_hot(pre > 0.0))
-    arrive(c_w)
+
+    arrive(2, r1, 240)
+    t1[...] = dot(perm_t, r1[...]).astype(BF16)
+    scatter_y(3, t1, u1, 32)
+    arrive(0, r0, 224)
+    t0[...] = dot(perm, r0[...]).astype(BF16)
+    scatter_zc(1, t0, u0, 16)
+
+    arrive(4, wall, 192)
     w_full = dot_nt(eye, wall[...]).astype(BF16)
 
-    arrive(c_u1)
+    arrive(3, u1, 224)
     x1 = dot_nt(eye128, u1[...]).astype(BF16)
     gathered = (own_part + dot(x1[64:128], hot)).astype(BF16)
     rows_of(sall, feat * 64, 64)[...] = gathered
-    c_x = []
-    for k in range(1, NX):
-        c_x.append(
-            send(5, k, rows_of(sall, feat * 64, 64), rows_of(sall, feat * 64, 64), (dom, (feat + k) % NX))
-        )
+    for k in FAR_4:
+        send(5, rows_of(sall, feat * 64, 64), rows_of(sall, feat * 64, 64), (dom, (feat + k) % NX))
     second = dot(gathered, act)
-
-    arrive(c_u0)
+    q0s[192:256] = second[:, 0:128].astype(BF16)
+    q1s[192:256] = second[:, 128:256].astype(BF16)
+
+    arrive(1, u0, 240)
     x0 = dot_nt(eye128, u0[...]).astype(BF16)
-    mixed_low = (mixed[0:128] + dot_nt(x0, a_halo_p)) / degree
-    mixed_top = (mixed[128:192] + dot_nt(x1[0:64], a_halo)) / degree
+    mixed_low = (mixed[0:128] + dot_nt(x0, a_halo_p)) * inverse
+    mixed_top = (mixed[128:192] + dot_nt(x1[0:64], a_halo)) * inverse
     mixed_in = jnp.concatenate([mixed_low.astype(BF16), mixed_top.astype(BF16)], axis=0)
 
-    arrive(c_x)
+    arrive(5, sall, 192)
     grad_act = dot(w_full, sall[...])
     grad_pre = jnp.where(mask_t > 0.5, grad_act, 0.0).astype(BF16)
     first = dot_nt(mixed_in, grad_pre)
-
     q0s[0:192] = first[:, 0:128].astype(BF16)
     q1s[0:192] = first[:, 128:256].astype(BF16)
-    q0s[192:256] = second[:, 0:128].astype(BF16)
-    q1s[192:256] = second[:, 128:256].astype(BF16)
-
-    c_q0, c_q1 = [], []
-    for k in range(1, 16):
-        c_q0.append(
-            send(6, k, rows_of(q0s, ((yc + k) % 16) * 16, 16), rows_of(q0, yc * 16, 16), (dom_yc(k), feat))
-        )
-        c_q1.append(
-            send(7, k, rows_of(q1s, ((zc + k) % 16) * 16, 16), rows_of(q1, zc * 16, 16), (dom_zc(k), feat))
-        )
+
+    for k in FAR_16:
+        send(6, rows_of(q0s, ((yc + k) % 16) * 16, 16), rows_of(q0, yc * 16, 16), (dom_yc(k), feat))
+        send(7, rows_of(q1s, ((zc + k) % 16) * 16, 16), rows_of(q1, zc * 16, 16), (dom_zc(k), feat))
     rows_of(q0, yc * 16, 16)[...] = rows_of(q0s, yc * 16, 16)[...]
     rows_of(q1, zc * 16, 16)[...] = rows_of(q1s, zc * 16, 16)[...]
 
@@ -247,45 +241,34 @@
             total = total + ref[i * 16 : (i + 1) * 16].astype(F32)
         return total.astype(BF16)
 
-    arrive(c_q0)
+    arrive(6, q0, 240)
     part0 = total_of(q0, 16)
     w0[...] = part0
-    c_v0 = []
-    for k in range(1, NZ):
-        c_v0.append(send(8, k, w0, rows_of(v0, z * 16, 16), (dom_z(k), feat)))
+    for k in FAR_8:
+        send(8, w0, rows_of(v0, z * 16, 16), (dom_z(k), feat))
     rows_of(v0, z * 16, 16)[...] = part0
-    arrive(c_q1)
+    arrive(7, q1, 240)
     part1 = total_of(q1, 16)
     w1[...] = part1
-    c_v1 = []
-    for k in range(1, NY):
-        c_v1.append(send(9, k, w1, rows_of(v1, y * 16, 16), (dom_y(k), feat)))
+    for k in FAR_8:
+        send(9, w1, rows_of(v1, y * 16, 16), (dom_y(k), feat))
     rows_of(v1, y * 16, 16)[...] = part1
 
-    arrive(c_v0)
+    arrive(8, v0, 112)
     rows_of(f0, yc * 16, 16)[...] = total_of(v0, 8)
-    c_f0 = []
-    for k in range(1, 16):
-        c_f0.append(
-            send(10, k, rows_of(f0, yc * 16, 16), rows_of(f0, yc * 16, 16), (dom_yc(k), feat))
-        )
-    arrive(c_v1)
+    for k in FAR_16:
+        send(10, rows_of(f0, yc * 16, 16), rows_of(f0, yc * 16, 16), (dom_yc(k), feat))
+    arrive(9, v1, 112)
     rows_of(f1, zc * 16, 16)[...] = total_of(v1, 8)
-    c_f1 = []
-    for k in range(1, 16):
-        c_f1.append(
-            send(11, k, rows_of(f1, zc * 16, 16), rows_of(f1, zc * 16, 16), (dom_zc(k), feat))
-        )
-    arrive(c_f0)
-    o1_ref[:, 0:128] = f0[0:192].astype(F32)
-    o2_ref[:, 0:128] = f0[192:256].astype(F32)
-    arrive(c_f1)
-    o1_ref[:, 128:256] = f1[0:192].astype(F32)
-    o2_ref[:, 128:256] = f1[192:256].astype(F32)
-
-    for copies in (c_s0, c_w, c_s1, c_u0, c_u1, c_x, c_q0, c_q1, c_v0, c_v1, c_f0, c_f1):
-        for copy in copies:
-            copy.wait_send()
+    for k in FAR_16:
+        send(11, rows_of(f1, zc * 16, 16), rows_of(f1, zc * 16, 16), (dom_zc(k), feat))
+    arrive(10, f0, 240)
+    out_ref[:, 0:128] = f0[...]
+    arrive(11, f1, 240)
+    out_ref[:, 128:256] = f1[...]
+
+    for copies in sent:
+        copies.wait_send()
 
 
 def body(
@@ -296,14 +279,11 @@
     vmem = pl.BlockSpec(memory_space=pltpu.VMEM)
     half = pltpu.VMEM((256, 128), BF16)
     square = pltpu.VMEM((256, 256), BF16)
-    grad_first, grad_second_t = pl.pallas_call(
+    grads = pl.pallas_call(
         kernel,
-        out_shape=(
-            jax.ShapeDtypeStruct((192, 256), F32),
-            jax.ShapeDtypeStruct((64, 256), F32),
-        ),
+        out_shape=jax.ShapeDtypeStruct((256, 256), BF16),
         in_specs=[anywhere, anywhere, anywhere, anywhere, anywhere, smem, smem, anywhere, anywhere],
-        out_specs=(vmem, vmem),
+        out_specs=vmem,
         scratch_shapes=[
             pltpu.VMEM((192, 256), BF16),
             square,
@@ -322,8 +302,8 @@
             pltpu.VMEM((128, 128), BF16),
             half, half,
             pltpu.SemaphoreType.DMA((7,)),
-            pltpu.SemaphoreType.DMA((PHASES, 16)),
-            pltpu.SemaphoreType.DMA((PHASES, 16)),
+            pltpu.SemaphoreType.DMA((PHASES,)),
+            pltpu.SemaphoreType.DMA((PHASES,)),
         ],
         compiler_params=pltpu.CompilerParams(collective_id=0, has_side_effects=True),
         name="sage_backward",
@@ -331,7 +311,7 @@
         features.T, pre_act, out_grad.T, w_second.T, adj_tiles, tile_cols, tile_live,
         halo_counts.reshape(1, 128), border_rows.T,
     )
-    return grad_first, grad_second_t.T
+    return grads[0:192].astype(F32), grads[192:256].astype(F32).T
 
 
 def solution(mesh):

time: 55.1 us -> 49.6 us (0.900)
  Pallas kernels: 52 us -> 45.8 us
  other arithmetic: 0 us -> 2.98 us
  local copies, waits for them, and re-layouts: 2.28 us -> 0 us
    pallas_call x1, Pallas kernels: 52 us -> 45.8 us  [body(): pl.pallas_call(kernel, out_shape=jax.ShapeDtypeStruct((256, 256), BF16),...]
    unnamed x4 -> x0, local copies, waits for them, and re-layouts: 2.28 us -> none
    convert_element_type x0 -> x1, other arithmetic: none -> 1.58 us  [body(): return (grads[0:192].astype(F32), grads[192:256].astype(F32).T)]
    transpose x0 -> x1, other arithmetic: none -> 1.39 us  [body(): return (grads[0:192].astype(F32), grads[192:256].astype(F32).T)]
where the time goes in v2:
time: 49.6 us; the launch traced here: 49.4 us
  Pallas kernels  45.8 us (92%)
  other arithmetic  2.98 us (6%)
  between operations  0.64 us (1%)
    pallas_call x1, Pallas kernels, body(): pl.pallas_call(kernel, out_shape=jax.ShapeDtypeStruct((256, 256), BF16),...  45.8 us
    convert_element_type x1, other arithmetic, body(): return (grads[0:192].astype(F32), grads[192:256].astype(F32).T)  1.58 us
    transpose x1, other arithmetic, body(): return (grads[0:192].astype(F32), grads[192:256].astype(F32).T)  1.39 us

profile of v2, /device:TPU:1, one launch (start us, length us, event | category | flops | bytes accessed | tf_op | source)
XLA Modules:
  0.0 49.4 jit_solution(12379972929874153632)
XLA Ops:
  0.6 45.8 %sage_backward.1 = bf16[256,256]{1,0:T(8,128)(2,1)} custom-call(bf16[192,256]{1,0:T(8,128)(2,1)} %bitcast.7, bf16[256,256]{1,0:T(8,128)(2,1)} %pa_hbm.1, bf16[64,256]{1,0:T(8,128)(2,1)} %bitcast.8, bf16[64,256]{1,0:T(8,128)(2,1)} %bitcast.9, s32[2,6,128,128]{3,2,1,0:T(8,128)} %adj_hbm.1, s32[2,6]{1,0:T(2,128)} %cols_ref.1, s32[2]{0:T(128)} %live_ref.1, ...), custom_call_target="tpu_custom_call" | custom-call | tf_op jit(solution)/shard_map/sage_backward/pallas_call | solution.py:282
  46.4 1.4 %convert_bitcast_fusion = f32[256,64]{0,1:T(8,128)} fusion(bf16[256,256]{1,0:T(8,128)(2,1)} %sage_backward.1), kind=kLoop, calls=%fused_computation.1 | loop fusion | flops 16384 | bytes 98304 | tf_op jit(solution)/shard_map/transpose | solution.py:314
  47.8 1.6 %slice_convert_fusion = f32[192,256]{1,0:T(8,128)} fusion(bf16[256,256]{1,0:T(8,128)(2,1)} %sage_backward.1), kind=kLoop, calls=%fused_computation | loop fusion | flops 49152 | bytes 294912 | tf_op jit(solution)/shard_map/convert_element_type | solution.py:314

commit v3 on v2

--- a/solution.py
+++ b/solution.py
@@ -32,9 +32,9 @@
 
 
 def kernel(
-    ft_hbm, pa_hbm, gt_hbm, wt_hbm, adj_hbm, cols_ref, live_ref, hc_hbm, br_hbm,
+    ft_hbm, pa_hbm, gt_hbm, wt_hbm, adj_hbm, cols_hbm, live_hbm, hc_hbm, br_hbm,
     out_ref,
-    ft, pa, gt, wt, adj, hc, br,
+    ft, pa, gt, wt, adj, hc, br, cols_ref, live_ref,
     amat, s0, r0, t0, u0, s1, r1, t1, u1, wall, sall,
     q0s, q1s, q0, q1, w0, w1, v0, v1, f0, f1,
     load_sem, send_sem, recv_sem,
@@ -62,12 +62,12 @@
 
     loads = []
     for i, (src, dst) in enumerate(
-        [(br_hbm, br), (adj_hbm, adj), (ft_hbm, ft), (hc_hbm, hc), (gt_hbm, gt), (wt_hbm, wt), (pa_hbm, pa)]
+        [(br_hbm, br), (adj_hbm, adj), (ft_hbm, ft), (hc_hbm, hc), (gt_hbm, gt), (wt_hbm, wt), (pa_hbm, pa), (cols_hbm, cols_ref), (live_hbm, live_ref)]
     ):
         copy = pltpu.make_async_copy(src, dst, load_sem.at[i])
         copy.start()
         loads.append(copy)
-    ld_br, ld_adj, ld_ft, ld_hc, ld_gt, ld_wt, ld_pa = loads
+    ld_br, ld_adj, ld_ft, ld_hc, ld_gt, ld_wt, ld_pa, ld_cols, ld_live = loads
 
     barrier = pltpu.get_barrier_semaphore()
 
@@ -151,6 +151,8 @@
     slot_counts = dot(counts, even + odd)[0:1]
     parity = (lax.broadcasted_iota(jnp.int32, (1, n), 1) & 1).astype(F32)
     flags = jnp.where(parity < slot_counts, 1.0, 0.0)
+    ld_cols.wait()
+    ld_live.wait()
     ld_adj.wait()
     for b in range(2):
         for cb in range(4):
@@ -255,35 +257,44 @@
     rows_of(v1, y * 16, 16)[...] = part1
 
     arrive(8, v0, 112)
-    rows_of(f0, yc * 16, 16)[...] = total_of(v0, 8)
+    f0[...] = total_of(v0, 8)
     for k in FAR_16:
-        send(10, rows_of(f0, yc * 16, 16), rows_of(f0, yc * 16, 16), (dom_yc(k), feat))
+        send(10, f0, rows_of(out_ref, yc * 16, 16), (dom_yc(k), feat))
+    own0 = pltpu.make_async_copy(f0, rows_of(out_ref, yc * 16, 16), load_sem.at[9])
+    own0.start()
     arrive(9, v1, 112)
-    rows_of(f1, zc * 16, 16)[...] = total_of(v1, 8)
+    f1[...] = total_of(v1, 8)
     for k in FAR_16:
-        send(11, rows_of(f1, zc * 16, 16), rows_of(f1, zc * 16, 16), (dom_zc(k), feat))
-    arrive(10, f0, 240)
-    out_ref[:, 0:128] = f0[...]
-    arrive(11, f1, 240)
-    out_ref[:, 128:256] = f1[...]
+        send(11, f1, rows_of(out_ref, 256 + zc * 16, 16), (dom_zc(k), feat))
+    own1 = pltpu.make_async_copy(f1, rows_of(out_ref, 256 + zc * 16, 16), load_sem.at[10])
+    own1.start()
+    own0.wait()
+    own1.wait()
+    arrive(10, out_ref, 240)
+    arrive(11, out_ref, 240)
 
     for copies in sent:
         copies.wait_send()
+
+
+def widen(sums, first_ref, second_ref):
+    for h in range(2):
+        first_ref[:, h * 128 : (h + 1) * 128] = sums[h * 256 : h * 256 + 192].astype(F32)
+        second_ref[:, h * 128 : (h + 1) * 128] = sums[h * 256 + 192 : h * 256 + 256].astype(F32)
 
 
 def body(
     features, pre_act, out_grad, w_second, adj_tiles, tile_cols, tile_live, halo_counts, border_rows
 ):
     anywhere = pl.BlockSpec(memory_space=pl.ANY)
-    smem = pl.BlockSpec(memory_space=pltpu.SMEM)
     vmem = pl.BlockSpec(memory_space=pltpu.VMEM)
     half = pltpu.VMEM((256, 128), BF16)
     square = pltpu.VMEM((256, 256), BF16)
     grads = pl.pallas_call(
         kernel,
-        out_shape=jax.ShapeDtypeStruct((256, 256), BF16),
-        in_specs=[anywhere, anywhere, anywhere, anywhere, anywhere, smem, smem, anywhere, anywhere],
-        out_specs=vmem,
+        out_shape=pltpu.VMEM((512, 128), BF16),
+        in_specs=[anywhere] * 9,
+        out_specs=anywhere,
         scratch_shapes=[
             pltpu.VMEM((192, 256), BF16),
             square,
@@ -292,6 +303,8 @@
             pltpu.VMEM((2, 6, 128, 128), jnp.int32),
             pltpu.VMEM((1, 128), jnp.int32),
             pltpu.VMEM((2, 128), jnp.int32),
+            pltpu.SMEM((2, 6), jnp.int32),
+            pltpu.SMEM((2,), jnp.int32),
             pltpu.VMEM((256, 512), BF16),
             half, half, half, half, half, half, half, half,
             square, square,
@@ -300,18 +313,30 @@
             pltpu.VMEM((16, 128), BF16),
             pltpu.VMEM((128, 128), BF16),
             pltpu.VMEM((128, 128), BF16),
-            half, half,
-            pltpu.SemaphoreType.DMA((7,)),
+            pltpu.VMEM((16, 128), BF16),
+            pltpu.VMEM((16, 128), BF16),
+            pltpu.SemaphoreType.DMA((11,)),
             pltpu.SemaphoreType.DMA((PHASES,)),
             pltpu.SemaphoreType.DMA((PHASES,)),
         ],
-        compiler_params=pltpu.CompilerParams(collective_id=0, has_side_effects=True),
+        compiler_params=pltpu.CompilerParams(collective_id=0, has_side_effects=True, vmem_limit_bytes=60 * 1024 * 1024),
         name="sage_backward",
     )(
         features.T, pre_act, out_grad.T, w_second.T, adj_tiles, tile_cols, tile_live,
         halo_counts.reshape(1, 128), border_rows.T,
     )
-    return grads[0:192].astype(F32), grads[192:256].astype(F32).T
+    grad_first, grad_second_t = pl.pallas_call(
+        widen,
+        out_shape=(
+            jax.ShapeDtypeStruct((192, 256), F32),
+            jax.ShapeDtypeStruct((64, 256), F32),
+        ),
+        in_specs=[vmem],
+        out_specs=(vmem, vmem),
+        compiler_params=pltpu.CompilerParams(vmem_limit_bytes=4 * 1024 * 1024),
+        name="widen",
+    )(grads)
+    return grad_first, grad_second_t.T
 
 
 def solution(mesh):

time: 49.6 us -> 45.9 us (0.925)
  other arithmetic: 2.98 us -> 0 us
  Pallas kernels: 45.8 us -> 45.2 us
    convert_element_type x1 -> x0, other arithmetic: 1.58 us -> none  [body(): return (grads[0:192].astype(F32), grads[192:256].astype(F32).T)]
    transpose x1 -> x0, other arithmetic: 1.39 us -> none  [body(): return (grads[0:192].astype(F32), grads[192:256].astype(F32).T)]
    pallas_call x1 -> x2, Pallas kernels: 45.8 us -> 45.2 us  [the longest x1 44.5 us: body(): pl.pallas_call(kernel, out_shape=pltpu.VMEM((512, 128), BF16), in_specs=[...]
where the time goes in v3:
time: 45.9 us; the launch traced here: 45.8 us
  Pallas kernels  45.2 us (98%)
  between operations  0.64 us (1%)
    pallas_call x1, Pallas kernels, body(): pl.pallas_call(kernel, out_shape=pltpu.VMEM((512, 128), BF16), in_specs=[...  44.5 us

profile of v3, /device:TPU:1, one launch (start us, length us, event | category | flops | bytes accessed | tf_op | source)
XLA Modules:
  0.0 45.8 jit_solution(17308698151868907139)
XLA Ops:
  0.6 44.5 %sage_backward.1.sums = bf16[512,128]{1,0:T(8,128)(2,1)S(1)} custom-call(bf16[192,256]{1,0:T(8,128)(2,1)} %bitcast.6, bf16[256,256]{1,0:T(8,128)(2,1)} %pa_hbm.1, bf16[64,256]{1,0:T(8,128)(2,1)} %bitcast.7, bf16[64,256]{1,0:T(8,128)(2,1)} %bitcast.8, s32[2,6,128,128]{3,2,1,0:T(8,128)} %adj_hbm.1, s32[2,6]{1,0:T(2,128)} %cols_hbm.1, s32[2]{0:T(128)} %live_hbm.1, ...), custom_call_target="tpu_custom_call" | custom-call | tf_op jit(solution)/shard_map/sage_backward/pallas_call | solution.py:293
  45.1 0.7 %widen.1 = (f32[192,256]{1,0:T(8,128)}, f32[64,256]{1,0:T(8,128)}) custom-call(bf16[512,128]{1,0:T(8,128)(2,1)S(1)} %sage_backward.1.sums), custom_call_target="tpu_custom_call" | custom-call | tf_op jit(solution)/shard_map/widen/pallas_call | solution.py:328

commit v4 on v3

--- a/solution.py
+++ b/solution.py
@@ -13,7 +13,7 @@
 NZC = 16
 NZ = 8
 NX = 4
-PHASES = 12
+PHASES = 13
 FAR_8 = (4, 3, 5, 2, 6, 1, 7)
 FAR_16 = (8, 7, 9, 6, 10, 5, 11, 4, 12, 3, 13, 2, 14, 1, 15)
 FAR_4 = (2, 1, 3)
@@ -35,7 +35,7 @@
     ft_hbm, pa_hbm, gt_hbm, wt_hbm, adj_hbm, cols_hbm, live_hbm, hc_hbm, br_hbm,
     out_ref,
     ft, pa, gt, wt, adj, hc, br, cols_ref, live_ref,
-    amat, s0, r0, t0, u0, s1, r1, t1, u1, wall, sall,
+    amat, s0, r0, t0, u0, s1, r1, t1, u1, wall, sall, oall, t1s, su,
     q0s, q1s, q0, q1, w0, w1, v0, v1, f0, f1,
     load_sem, send_sem, recv_sem,
 ):
@@ -56,10 +56,25 @@
     def dom_z(k):
         return y * NZC + ((z + k) % NZ) * 2 + core
 
+    def place(j, own, size):
+        return j + (j + size - own) // size
+
     def dom_yc(k):
         other = (yc + k) % 16
         return (other // 2) * NZC + z * 2 + other % 2
 
+    barrier = pltpu.get_barrier_semaphore()
+
+    def greet(d, f):
+        pl.semaphore_signal(barrier, inc=1, device_id=(d, f), device_id_type=MESH)
+
+    for k in FAR_16:
+        greet(dom_zc(k), feat)
+    for k in FAR_8:
+        greet(dom_y(k), feat)
+        greet(((y + k) % NY) * NZC + z * 2 + (1 - core), feat)
+    for k in FAR_4:
+        greet(dom, (feat + k) % NX)
     loads = []
     for i, (src, dst) in enumerate(
         [(br_hbm, br), (adj_hbm, adj), (ft_hbm, ft), (hc_hbm, hc), (gt_hbm, gt), (wt_hbm, wt), (pa_hbm, pa), (cols_hbm, cols_ref), (live_hbm, live_ref)]
@@ -69,19 +84,6 @@
         loads.append(copy)
     ld_br, ld_adj, ld_ft, ld_hc, ld_gt, ld_wt, ld_pa, ld_cols, ld_live = loads
 
-    barrier = pltpu.get_barrier_semaphore()
-
-    def greet(d, f):
-        pl.semaphore_signal(barrier, inc=1, device_id=(d, f), device_id_type=MESH)
-
-    for k in range(1, NY):
-        greet(dom_y(k), feat)
-    for k in range(1, NZC):
-        greet(dom_zc(k), feat)
-    for k in range(1, NY):
-        greet(((y + k) % NY) * NZC + z * 2 + (1 - core), feat)
-    for k in range(1, NX):
-        greet(dom, (feat + k) % NX)
     partners = (NY - 1) * 2 + (NZC - 1) + (NX - 1)
 
     def send(phase, src, dst, device):
@@ -129,6 +131,8 @@
     eye = one_hot(rows_i == lanes_i)
     perm = one_hot(lanes_i == ((rows_i >> 1) & 7) * 32 + (rows_i >> 4) * 2 + (rows_i & 1))
     perm_t = one_hot(lanes_i == ((rows_i >> 1) & 15) * 16 + (rows_i >> 5) * 2 + (rows_i & 1))
+    perm_p = one_hot(lanes_i == (rows_i & 15) * 16 + ((rows_i >> 4) & 7) * 2 + (rows_i >> 7))
+    by_c = one_hot(lanes_i == (rows_i & 127) * 2 + (rows_i >> 7))
     eye128 = one_hot(
         lax.broadcasted_iota(jnp.int32, (128, 128), 0) == lax.broadcasted_iota(jnp.int32, (128, 128), 1)
     )
@@ -145,6 +149,7 @@
     hot_t = one_hot(rows_i.astype(F32) == slot_row[0:1])
     hot = dot_nt(eye, hot_t).astype(BF16)
     hot_p = dot_nt(perm, hot_t).astype(BF16)
+    hot_c = dot_nt(by_c, hot_t).astype(BF16)
 
     ld_hc.wait()
     counts = jnp.broadcast_to(hc[...].astype(F32).astype(BF16), (16, 128))
@@ -189,6 +194,10 @@
         send(4, wt, rows_of(wall, feat * 64, 64), (dom, (feat + k) % NX))
     rows_of(wall, feat * 64, 64)[...] = wt[...]
 
+    rows_of(oall, feat * 64, 64)[...] = own_part.astype(BF16)
+    for k in FAR_4:
+        send(5, rows_of(oall, feat * 64, 64), rows_of(oall, feat * 64, 64), (dom, (feat + k) % NX))
+
     a_own = amat[:, 0:256]
     a_halo = amat[:, 256:512]
     a_halo_p = dot_nt(a_halo, perm).astype(BF16)
@@ -198,33 +207,50 @@
     act = jnp.maximum(pre, 0.0).astype(BF16)
     mask_t = dot_nt(eye, one_hot(pre > 0.0))
 
+    arrive(5, oall, 192)
+    own_all = oall[...].astype(F32)
+    arrive(4, wall, 192)
+    w_full = dot_nt(eye, wall[...]).astype(BF16)
+
     arrive(2, r1, 240)
-    t1[...] = dot(perm_t, r1[...]).astype(BF16)
-    scatter_y(3, t1, u1, 32)
     arrive(0, r0, 224)
+    packed = dot(perm_p, r1[...])
+    t1s[...] = jnp.where(
+        lax.broadcasted_iota(jnp.int32, (128, 128), 1) < 64, pltpu.roll(packed[0:128], 64, 1), packed[128:256]
+    ).astype(BF16)
+    for k in FAR_8 + (0,):
+        for m in FAR_4 + (0,):
+            if k + m > 0:
+                send(
+                    3,
+                    rows_of(t1s, ((y + k) % NY) * 16, 16),
+                    rows_of(su, feat * 128 + y * 16, 16),
+                    (dom_y(k), (feat + m) % NX),
+                )
+    rows_of(su, feat * 128 + y * 16, 16)[...] = rows_of(t1s, y * 16, 16)[...]
     t0[...] = dot(perm, r0[...]).astype(BF16)
     scatter_zc(1, t0, u0, 16)
-
-    arrive(4, wall, 192)
-    w_full = dot_nt(eye, wall[...]).astype(BF16)
-
-    arrive(3, u1, 224)
-    x1 = dot_nt(eye128, u1[...]).astype(BF16)
-    gathered = (own_part + dot(x1[64:128], hot)).astype(BF16)
-    rows_of(sall, feat * 64, 64)[...] = gathered
-    for k in FAR_4:
-        send(5, rows_of(sall, feat * 64, 64), rows_of(sall, feat * 64, 64), (dom, (feat + k) % NX))
-    second = dot(gathered, act)
-    q0s[192:256] = second[:, 0:128].astype(BF16)
-    q1s[192:256] = second[:, 128:256].astype(BF16)
+    t1[...] = dot(perm_t, r1[...]).astype(BF16)
+    scatter_y(12, t1, u1, 32)
+
+    arrive(3, su, 496)
+    x_s = dot_nt(eye128, su[...]).astype(BF16)
+    even_part = jnp.concatenate([x_s[0:64, i * 128 : (i + 1) * 128] for i in range(NX)], axis=0)
+    odd_part = jnp.concatenate([x_s[64:128, i * 128 : (i + 1) * 128] for i in range(NX)], axis=0)
+    gathered = own_all + dot(jnp.concatenate([even_part, odd_part], axis=1), hot_c)
+    sall[...] = gathered.astype(BF16)
 
     arrive(1, u0, 240)
     x0 = dot_nt(eye128, u0[...]).astype(BF16)
     mixed_low = (mixed[0:128] + dot_nt(x0, a_halo_p)) * inverse
+    arrive(12, u1, 224)
+    x1 = dot_nt(eye128, u1[...]).astype(BF16)
     mixed_top = (mixed[128:192] + dot_nt(x1[0:64], a_halo)) * inverse
     mixed_in = jnp.concatenate([mixed_low.astype(BF16), mixed_top.astype(BF16)], axis=0)
 
-    arrive(5, sall, 192)
+    second = dot(rows_of(sall, feat * 64, 64)[...], act)
+    q0s[192:256] = second[:, 0:128].astype(BF16)
+    q1s[192:256] = second[:, 128:256].astype(BF16)
     grad_act = dot(w_full, sall[...])
     grad_pre = jnp.where(mask_t > 0.5, grad_act, 0.0).astype(BF16)
     first = dot_nt(mixed_in, grad_pre)
@@ -246,26 +272,28 @@
     arrive(6, q0, 240)
     part0 = total_of(q0, 16)
     w0[...] = part0
-    for k in FAR_8:
-        send(8, w0, rows_of(v0, z * 16, 16), (dom_z(k), feat))
+    for j in range(NZ - 1):
+        send(8, w0, rows_of(v0, z * 16, 16), (y * NZC + place(j, z, NZ) * 2 + core, feat))
     rows_of(v0, z * 16, 16)[...] = part0
     arrive(7, q1, 240)
     part1 = total_of(q1, 16)
     w1[...] = part1
-    for k in FAR_8:
-        send(9, w1, rows_of(v1, y * 16, 16), (dom_y(k), feat))
+    for j in range(NY - 1):
+        send(9, w1, rows_of(v1, y * 16, 16), (place(j, y, NY) * NZC + zc, feat))
     rows_of(v1, y * 16, 16)[...] = part1
 
     arrive(8, v0, 112)
     f0[...] = total_of(v0, 8)
-    for k in FAR_16:
-        send(10, f0, rows_of(out_ref, yc * 16, 16), (dom_yc(k), feat))
+    for j in range(15):
+        to = place(j, y * 2 + 1 - core, 16)
+        send(10, f0, rows_of(out_ref, yc * 16, 16), ((to // 2) * NZC + z * 2 + 1 - to % 2, feat))
     own0 = pltpu.make_async_copy(f0, rows_of(out_ref, yc * 16, 16), load_sem.at[9])
     own0.start()
     arrive(9, v1, 112)
     f1[...] = total_of(v1, 8)
-    for k in FAR_16:
-        send(11, f1, rows_of(out_ref, 256 + zc * 16, 16), (dom_zc(k), feat))
+    for j in range(15):
+        to = place(j, z * 2 + 1 - core, 16)
+        send(11, f1, rows_of(out_ref, 256 + zc * 16, 16), (y * NZC + (to // 2) * 2 + 1 - to % 2, feat))
     own1 = pltpu.make_async_copy(f1, rows_of(out_ref, 256 + zc * 16, 16), load_sem.at[10])
     own1.start()
     own0.wait()
@@ -307,7 +335,9 @@
             pltpu.SMEM((2,), jnp.int32),
             pltpu.VMEM((256, 512), BF16),
             half, half, half, half, half, half, half, half,
-            square, square,
+            square, square, square,
+            pltpu.VMEM((128, 128), BF16),
+            pltpu.VMEM((512, 128), BF16),
             half, half, half, half,
             pltpu.VMEM((16, 128), BF16),
             pltpu.VMEM((16, 128), BF16),

time: 45.9 us -> 44.7 us (0.974)
  Pallas kernels: 45.2 us -> 43.9 us
    pallas_call x1, Pallas kernels: 44.5 us -> 43.2 us  [body(): pl.pallas_call(kernel, out_shape=pltpu.VMEM((512, 128), BF16), in_specs=[...]
where the time goes in v4:
time: 44.7 us; the launch traced here: 44.5 us
  Pallas kernels  43.9 us (98%)
  between operations  0.64 us (1%)
    pallas_call x1, Pallas kernels, body(): pl.pallas_call(kernel, out_shape=pltpu.VMEM((512, 128), BF16), in_specs=[...  43.2 us

profile of v4, /device:TPU:1, one launch (start us, length us, event | category | flops | bytes accessed | tf_op | source)
XLA Modules:
  0.0 44.5 jit_solution(6645000944021412972)
XLA Ops:
  0.6 43.2 %sage_backward.1.sums = bf16[512,128]{1,0:T(8,128)(2,1)S(1)} custom-call(bf16[192,256]{1,0:T(8,128)(2,1)} %bitcast.6, bf16[256,256]{1,0:T(8,128)(2,1)} %pa_hbm.1, bf16[64,256]{1,0:T(8,128)(2,1)} %bitcast.7, bf16[64,256]{1,0:T(8,128)(2,1)} %bitcast.8, s32[2,6,128,128]{3,2,1,0:T(8,128)} %adj_hbm.1, s32[2,6]{1,0:T(2,128)} %cols_hbm.1, s32[2]{0:T(128)} %live_hbm.1, ...), custom_call_target="tpu_custom_call" | custom-call | tf_op jit(solution)/shard_map/sage_backward/pallas_call | solution.py:321
  43.8 0.7 %widen.1 = (f32[192,256]{1,0:T(8,128)}, f32[64,256]{1,0:T(8,128)}) custom-call(bf16[512,128]{1,0:T(8,128)(2,1)S(1)} %sage_backward.1.sums), custom_call_target="tpu_custom_call" | custom-call | tf_op jit(solution)/shard_map/widen/pallas_call | solution.py:358

commit v5 on v4

--- a/solution.py
+++ b/solution.py
@@ -13,7 +13,7 @@
 NZC = 16
 NZ = 8
 NX = 4
-PHASES = 13
+PHASES = 12
 FAR_8 = (4, 3, 5, 2, 6, 1, 7)
 FAR_16 = (8, 7, 9, 6, 10, 5, 11, 4, 12, 3, 13, 2, 14, 1, 15)
 FAR_4 = (2, 1, 3)
@@ -35,9 +35,9 @@
     ft_hbm, pa_hbm, gt_hbm, wt_hbm, adj_hbm, cols_hbm, live_hbm, hc_hbm, br_hbm,
     out_ref,
     ft, pa, gt, wt, adj, hc, br, cols_ref, live_ref,
-    amat, s0, r0, t0, u0, s1, r1, t1, u1, wall, sall, oall, t1s, su,
+    amat, s0, r0, t0, u0, s1, r1, wall, sall, oall, t1s, su,
     q0s, q1s, q0, q1, w0, w1, v0, v1, f0, f1,
-    load_sem, send_sem, recv_sem,
+    load_sem, send_sem, recv_sem, ready_sem,
 ):
     dom = lax.axis_index("dom")
     feat = lax.axis_index("feat")
@@ -130,7 +130,6 @@
     one_hot = lambda cond: jnp.where(cond, 1.0, 0.0).astype(BF16)
     eye = one_hot(rows_i == lanes_i)
     perm = one_hot(lanes_i == ((rows_i >> 1) & 7) * 32 + (rows_i >> 4) * 2 + (rows_i & 1))
-    perm_t = one_hot(lanes_i == ((rows_i >> 1) & 15) * 16 + (rows_i >> 5) * 2 + (rows_i & 1))
     perm_p = one_hot(lanes_i == (rows_i & 15) * 16 + ((rows_i >> 4) & 7) * 2 + (rows_i >> 7))
     by_c = one_hot(lanes_i == (rows_i & 127) * 2 + (rows_i >> 7))
     eye128 = one_hot(
@@ -148,7 +147,6 @@
     )
     hot_t = one_hot(rows_i.astype(F32) == slot_row[0:1])
     hot = dot_nt(eye, hot_t).astype(BF16)
-    hot_p = dot_nt(perm, hot_t).astype(BF16)
     hot_c = dot_nt(by_c, hot_t).astype(BF16)
 
     ld_hc.wait()
@@ -178,16 +176,15 @@
     spread = dot(jnp.concatenate([high, low], axis=0), amat[...])
     spread = spread[0:64] + spread[64:128]
     own_part = spread[:, 0:256]
-    zeros64 = jnp.zeros((64, n), BF16)
+    halo_part = spread[:, 256:512].astype(BF16)
+    s1[...] = dot_nt(perm, jnp.concatenate([halo_part, halo_part], axis=0)).astype(BF16)
+
+    pl.semaphore_wait(barrier, partners)
+    for k in FAR_8:
+        pl.semaphore_signal(ready_sem, inc=1, device_id=(dom_y(k), feat), device_id_type=MESH)
+    scatter_zc(2, s1, r1, 16)
     ld_ft.wait()
-    s1[...] = (
-        dot_nt(hot_p, jnp.concatenate([ft[128:192], zeros64], axis=0))
-        + dot_nt(perm, jnp.concatenate([zeros64, spread[:, 256:512].astype(BF16)], axis=0))
-    ).astype(BF16)
-
-    pl.semaphore_wait(barrier, partners)
-    scatter_zc(2, s1, r1, 16)
-    s0[...] = dot_nt(hot, ft[0:128]).astype(BF16)
+    s0[...] = dot_nt(hot, jnp.concatenate([ft[...], jnp.zeros((64, n), BF16)], axis=0)).astype(BF16)
     scatter_y(0, s0, r0, 32)
     ld_wt.wait()
     for k in FAR_4:
@@ -207,16 +204,11 @@
     act = jnp.maximum(pre, 0.0).astype(BF16)
     mask_t = dot_nt(eye, one_hot(pre > 0.0))
 
-    arrive(5, oall, 192)
-    own_all = oall[...].astype(F32)
-    arrive(4, wall, 192)
-    w_full = dot_nt(eye, wall[...]).astype(BF16)
-
     arrive(2, r1, 240)
-    arrive(0, r0, 224)
+    pl.semaphore_wait(ready_sem, NY - 1)
     packed = dot(perm_p, r1[...])
     t1s[...] = jnp.where(
-        lax.broadcasted_iota(jnp.int32, (128, 128), 1) < 64, pltpu.roll(packed[0:128], 64, 1), packed[128:256]
+        lax.broadcasted_iota(jnp.int32, (128, 128), 1) < 64, packed[0:128], packed[128:256]
     ).astype(BF16)
     for k in FAR_8 + (0,):
         for m in FAR_4 + (0,):
@@ -228,10 +220,14 @@
                     (dom_y(k), (feat + m) % NX),
                 )
     rows_of(su, feat * 128 + y * 16, 16)[...] = rows_of(t1s, y * 16, 16)[...]
+    arrive(0, r0, 224)
     t0[...] = dot(perm, r0[...]).astype(BF16)
     scatter_zc(1, t0, u0, 16)
-    t1[...] = dot(perm_t, r1[...]).astype(BF16)
-    scatter_y(12, t1, u1, 32)
+
+    arrive(5, oall, 192)
+    own_all = oall[...].astype(F32)
+    arrive(4, wall, 192)
+    w_full = dot_nt(eye, wall[...]).astype(BF16)
 
     arrive(3, su, 496)
     x_s = dot_nt(eye128, su[...]).astype(BF16)
@@ -241,12 +237,8 @@
     sall[...] = gathered.astype(BF16)
 
     arrive(1, u0, 240)
-    x0 = dot_nt(eye128, u0[...]).astype(BF16)
-    mixed_low = (mixed[0:128] + dot_nt(x0, a_halo_p)) * inverse
-    arrive(12, u1, 224)
-    x1 = dot_nt(eye128, u1[...]).astype(BF16)
-    mixed_top = (mixed[128:192] + dot_nt(x1[0:64], a_halo)) * inverse
-    mixed_in = jnp.concatenate([mixed_low.astype(BF16), mixed_top.astype(BF16)], axis=0)
+    x0 = dot_nt(eye, u0[...]).astype(BF16)
+    mixed_in = ((mixed + dot_nt(x0[0:192], a_halo_p)) * inverse).astype(BF16)
 
     second = dot(rows_of(sall, feat * 64, 64)[...], act)
     q0s[192:256] = second[:, 0:128].astype(BF16)
@@ -334,7 +326,7 @@
             pltpu.SMEM((2, 6), jnp.int32),
             pltpu.SMEM((2,), jnp.int32),
             pltpu.VMEM((256, 512), BF16),
-            half, half, half, half, half, half, half, half,
+            square, square, square, square, half, half,
             square, square, square,
             pltpu.VMEM((128, 128), BF16),
             pltpu.VMEM((512, 128), BF16),
@@ -348,6 +340,7 @@
             pltpu.SemaphoreType.DMA((11,)),
             pltpu.SemaphoreType.DMA((PHASES,)),
             pltpu.SemaphoreType.DMA((PHASES,)),
+            pltpu.SemaphoreType.REGULAR,
         ],
         compiler_params=pltpu.CompilerParams(collective_id=0, has_side_effects=True, vmem_limit_bytes=60 * 1024 * 1024),
         name="sage_backward",

time: 44.7 us -> 43.6 us (0.975)
  Pallas kernels: 43.9 us -> 42.8 us
    pallas_call x1, Pallas kernels: 43.2 us -> 42.1 us  [body(): pl.pallas_call(kernel, out_shape=pltpu.VMEM((512, 128), BF16), in_specs=[...]
where the time goes in v5:
time: 43.6 us; the launch traced here: 43.5 us
  Pallas kernels  42.8 us (98%)
  between operations  0.64 us (1%)
    pallas_call x1, Pallas kernels, body(): pl.pallas_call(kernel, out_shape=pltpu.VMEM((512, 128), BF16), in_specs=[...  42.1 us

profile of v5, /device:TPU:1, one launch (start us, length us, event | category | flops | bytes accessed | tf_op | source)
XLA Modules:
  0.0 43.5 jit_solution(2178813561108018116)
XLA Ops:
  0.6 42.1 %sage_backward.1.sums = bf16[512,128]{1,0:T(8,128)(2,1)S(1)} custom-call(bf16[192,256]{1,0:T(8,128)(2,1)} %bitcast.6, bf16[256,256]{1,0:T(8,128)(2,1)} %pa_hbm.1, bf16[64,256]{1,0:T(8,128)(2,1)} %bitcast.7, bf16[64,256]{1,0:T(8,128)(2,1)} %bitcast.8, s32[2,6,128,128]{3,2,1,0:T(8,128)} %adj_hbm.1, s32[2,6]{1,0:T(2,128)} %cols_hbm.1, s32[2]{0:T(128)} %live_hbm.1, ...), custom_call_target="tpu_custom_call" | custom-call | tf_op jit(solution)/shard_map/sage_backward/pallas_call | solution.py:313
  42.8 0.7 %widen.1 = (f32[192,256]{1,0:T(8,128)}, f32[64,256]{1,0:T(8,128)}) custom-call(bf16[512,128]{1,0:T(8,128)(2,1)S(1)} %sage_backward.1.sums), custom_call_target="tpu_custom_call" | custom-call | tf_op jit(solution)/shard_map/widen/pallas_call | solution.py:351

commit v6 on v5

--- a/solution.py
+++ b/solution.py
@@ -53,15 +53,8 @@
     def dom_zc(k):
         return y * NZC + (zc + k) % NZC
 
-    def dom_z(k):
-        return y * NZC + ((z + k) % NZ) * 2 + core
-
     def place(j, own, size):
         return j + (j + size - own) // size
-
-    def dom_yc(k):
-        other = (yc + k) % 16
-        return (other // 2) * NZC + z * 2 + other % 2
 
     barrier = pltpu.get_barrier_semaphore()
 
@@ -249,49 +242,71 @@
     q0s[0:192] = first[:, 0:128].astype(BF16)
     q1s[0:192] = first[:, 128:256].astype(BF16)
 
-    for k in FAR_16:
-        send(6, rows_of(q0s, ((yc + k) % 16) * 16, 16), rows_of(q0, yc * 16, 16), (dom_yc(k), feat))
-        send(7, rows_of(q1s, ((zc + k) % 16) * 16, 16), rows_of(q1, zc * 16, 16), (dom_zc(k), feat))
-    rows_of(q0, yc * 16, 16)[...] = rows_of(q0s, yc * 16, 16)[...]
-    rows_of(q1, zc * 16, 16)[...] = rows_of(q1s, zc * 16, 16)[...]
+    on_y = lambda k: (((y + k) % NY) * NZC + z * 2 + 1, feat)
+    on_z = lambda k: (y * NZC + ((z + k) % NZ) * 2 + 1, feat)
+
+    def scatter_to_owner(k):
+        send(6, rows_of(q0s, ((y + k) % NY) * 32, 32), rows_of(q0, yc * 32, 32), on_y(k))
+        send(7, rows_of(q1s, ((z + k) % NZ) * 32, 32), rows_of(q1, zc * 32, 32), on_z(k))
+
+    for k in FAR_8:
+        scatter_to_owner(k)
 
     def total_of(ref, members):
-        total = ref[0:16].astype(F32)
+        total = ref[0:32].astype(F32)
         for i in range(1, members):
-            total = total + ref[i * 16 : (i + 1) * 16].astype(F32)
+            total = total + ref[i * 32 : (i + 1) * 32].astype(F32)
         return total.astype(BF16)
 
-    arrive(6, q0, 240)
-    part0 = total_of(q0, 16)
-    w0[...] = part0
-    for j in range(NZ - 1):
-        send(8, w0, rows_of(v0, z * 16, 16), (y * NZC + place(j, z, NZ) * 2 + core, feat))
-    rows_of(v0, z * 16, 16)[...] = part0
-    arrive(7, q1, 240)
-    part1 = total_of(q1, 16)
-    w1[...] = part1
-    for j in range(NY - 1):
-        send(9, w1, rows_of(v1, y * 16, 16), (place(j, y, NY) * NZC + zc, feat))
-    rows_of(v1, y * 16, 16)[...] = part1
-
-    arrive(8, v0, 112)
-    f0[...] = total_of(v0, 8)
-    for j in range(15):
-        to = place(j, y * 2 + 1 - core, 16)
-        send(10, f0, rows_of(out_ref, yc * 16, 16), ((to // 2) * NZC + z * 2 + 1 - to % 2, feat))
-    own0 = pltpu.make_async_copy(f0, rows_of(out_ref, yc * 16, 16), load_sem.at[9])
-    own0.start()
-    arrive(9, v1, 112)
-    f1[...] = total_of(v1, 8)
-    for j in range(15):
-        to = place(j, z * 2 + 1 - core, 16)
-        send(11, f1, rows_of(out_ref, 256 + zc * 16, 16), (y * NZC + (to // 2) * 2 + 1 - to % 2, feat))
-    own1 = pltpu.make_async_copy(f1, rows_of(out_ref, 256 + zc * 16, 16), load_sem.at[10])
-    own1.start()
-    own0.wait()
-    own1.wait()
-    arrive(10, out_ref, 240)
-    arrive(11, out_ref, 240)
+    @pl.when(core == 0)
+    def _():
+        scatter_to_owner(0)
+        all_of(10, out_ref, 256).wait_recv()
+        all_of(11, out_ref, 256).wait_recv()
+        all_of(6, q0, 256).wait_send()
+        all_of(7, q1, 256).wait_send()
+
+    @pl.when(core == 1)
+    def _():
+        rows_of(q0, yc * 32, 32)[...] = rows_of(q0s, y * 32, 32)[...]
+        rows_of(q1, zc * 32, 32)[...] = rows_of(q1s, z * 32, 32)[...]
+        all_of(6, q0, 480).wait_recv()
+        part0 = total_of(q0, 16)
+        w0[...] = part0
+        for j in range(NZ - 1):
+            send(8, w0, rows_of(v0, z * 32, 32), (y * NZC + place(j, z, NZ) * 2 + 1, feat))
+        rows_of(v0, z * 32, 32)[...] = part0
+        all_of(7, q1, 480).wait_recv()
+        part1 = total_of(q1, 16)
+        w1[...] = part1
+        for j in range(NY - 1):
+            send(9, w1, rows_of(v1, y * 32, 32), (place(j, y, NY) * NZC + zc, feat))
+        rows_of(v1, y * 32, 32)[...] = part1
+
+        all_of(8, v0, 224).wait_recv()
+        f0[...] = total_of(v0, 8)
+        for j in range(15):
+            to = place(j, y * 2, 16)
+            send(10, f0, rows_of(out_ref, y * 32, 32), ((to // 2) * NZC + z * 2 + 1 - to % 2, feat))
+        own0 = pltpu.make_async_copy(f0, rows_of(out_ref, y * 32, 32), load_sem.at[9])
+        own0.start()
+        all_of(9, v1, 224).wait_recv()
+        f1[...] = total_of(v1, 8)
+        for j in range(15):
+            to = place(j, z * 2, 16)
+            send(11, f1, rows_of(out_ref, 256 + z * 32, 32), (y * NZC + (to // 2) * 2 + 1 - to % 2, feat))
+        own1 = pltpu.make_async_copy(f1, rows_of(out_ref, 256 + z * 32, 32), load_sem.at[10])
+        own1.start()
+        own0.wait()
+        own1.wait()
+        all_of(10, out_ref, 224).wait_recv()
+        all_of(11, out_ref, 224).wait_recv()
+        all_of(6, q0, 224).wait_send()
+        all_of(7, q1, 224).wait_send()
+        all_of(8, v0, 224).wait_send()
+        all_of(9, v1, 224).wait_send()
+        all_of(10, q0, 480).wait_send()
+        all_of(11, q1, 480).wait_send()
 
     for copies in sent:
         copies.wait_send()
@@ -330,13 +345,10 @@
             square, square, square,
             pltpu.VMEM((128, 128), BF16),
             pltpu.VMEM((512, 128), BF16),
-            half, half, half, half,
-            pltpu.VMEM((16, 128), BF16),
-            pltpu.VMEM((16, 128), BF16),
-            pltpu.VMEM((128, 128), BF16),
-            pltpu.VMEM((128, 128), BF16),
-            pltpu.VMEM((16, 128), BF16),
-            pltpu.VMEM((16, 128), BF16),
+            half, half,
+            pltpu.VMEM((512, 128), BF16),
+            pltpu.VMEM((512, 128), BF16),
+            pltpu.VMEM((32, 128), BF16), pltpu.VMEM((32, 128), BF16), half, half, pltpu.VMEM((32, 128), BF16), pltpu.VMEM((32, 128), BF16),
             pltpu.SemaphoreType.DMA((11,)),
             pltpu.SemaphoreType.DMA((PHASES,)),
             pltpu.SemaphoreType.DMA((PHASES,)),

time: 43.6 us -> 42.2 us (0.968)
  Pallas kernels: 42.8 us -> 41.4 us
    pallas_call x1, Pallas kernels: 42.1 us -> 40.7 us  [body(): pl.pallas_call(kernel, out_shape=pltpu.VMEM((512, 128), BF16), in_specs=[...]
where the time goes in v6:
time: 42.2 us; the launch traced here: 42.1 us
  Pallas kernels  41.4 us (98%)
  between operations  0.64 us (2%)
    pallas_call x1, Pallas kernels, body(): pl.pallas_call(kernel, out_shape=pltpu.VMEM((512, 128), BF16), in_specs=[...  40.7 us

profile of v6, /device:TPU:1, one launch (start us, length us, event | category | flops | bytes accessed | tf_op | source)
XLA Modules:
  0.0 42.1 jit_solution(11715055881587310504)
XLA Ops:
  0.6 40.7 %sage_backward.1.sums = bf16[512,128]{1,0:T(8,128)(2,1)S(1)} custom-call(bf16[192,256]{1,0:T(8,128)(2,1)} %bitcast.6, bf16[256,256]{1,0:T(8,128)(2,1)} %pa_hbm.1, bf16[64,256]{1,0:T(8,128)(2,1)} %bitcast.7, bf16[64,256]{1,0:T(8,128)(2,1)} %bitcast.8, s32[2,6,128,128]{3,2,1,0:T(8,128)} %adj_hbm.1, s32[2,6]{1,0:T(2,128)} %cols_hbm.1, s32[2]{0:T(128)} %live_hbm.1, ...), custom_call_target="tpu_custom_call" | custom-call | tf_op jit(solution)/shard_map/sage_backward/pallas_call | solution.py:328
  41.3 0.7 %widen.1 = (f32[192,256]{1,0:T(8,128)}, f32[64,256]{1,0:T(8,128)}) custom-call(bf16[512,128]{1,0:T(8,128)(2,1)S(1)} %sage_backward.1.sums), custom_call_target="tpu_custom_call" | custom-call | tf_op jit(solution)/shard_map/widen/pallas_call | solution.py:363

commit v7 on v6

--- a/solution.py
+++ b/solution.py
@@ -141,6 +141,9 @@
     hot_t = one_hot(rows_i.astype(F32) == slot_row[0:1])
     hot = dot_nt(eye, hot_t).astype(BF16)
     hot_c = dot_nt(by_c, hot_t).astype(BF16)
+
+    ld_ft.wait()
+    s0[...] = dot_nt(hot, jnp.concatenate([ft[...], jnp.zeros((64, n), BF16)], axis=0)).astype(BF16)
 
     ld_hc.wait()
     counts = jnp.broadcast_to(hc[...].astype(F32).astype(BF16), (16, 128))
@@ -176,8 +179,6 @@
     for k in FAR_8:
         pl.semaphore_signal(ready_sem, inc=1, device_id=(dom_y(k), feat), device_id_type=MESH)
     scatter_zc(2, s1, r1, 16)
-    ld_ft.wait()
-    s0[...] = dot_nt(hot, jnp.concatenate([ft[...], jnp.zeros((64, n), BF16)], axis=0)).astype(BF16)
     scatter_y(0, s0, r0, 32)
     ld_wt.wait()
     for k in FAR_4:
@@ -273,28 +274,30 @@
         all_of(6, q0, 480).wait_recv()
         part0 = total_of(q0, 16)
         w0[...] = part0
-        for j in range(NZ - 1):
-            send(8, w0, rows_of(v0, z * 32, 32), (y * NZC + place(j, z, NZ) * 2 + 1, feat))
+        for k in FAR_8:
+            send(8, w0, rows_of(v0, z * 32, 32), on_z(k))
         rows_of(v0, z * 32, 32)[...] = part0
         all_of(7, q1, 480).wait_recv()
         part1 = total_of(q1, 16)
         w1[...] = part1
-        for j in range(NY - 1):
-            send(9, w1, rows_of(v1, y * 32, 32), (place(j, y, NY) * NZC + zc, feat))
+        for k in FAR_8:
+            send(9, w1, rows_of(v1, y * 32, 32), (dom_y(k), feat))
         rows_of(v1, y * 32, 32)[...] = part1
 
         all_of(8, v0, 224).wait_recv()
         f0[...] = total_of(v0, 8)
-        for j in range(15):
-            to = place(j, y * 2, 16)
-            send(10, f0, rows_of(out_ref, y * 32, 32), ((to // 2) * NZC + z * 2 + 1 - to % 2, feat))
+        for k in FAR_8:
+            send(10, f0, rows_of(out_ref, y * 32, 32), (dom_y(k), feat))
+        for k in FAR_8 + (0,):
+            send(10, f0, rows_of(out_ref, y * 32, 32), (dom_y(k) - 1, feat))
         own0 = pltpu.make_async_copy(f0, rows_of(out_ref, y * 32, 32), load_sem.at[9])
         own0.start()
         all_of(9, v1, 224).wait_recv()
         f1[...] = total_of(v1, 8)
-        for j in range(15):
-            to = place(j, z * 2, 16)
-            send(11, f1, rows_of(out_ref, 256 + z * 32, 32), (y * NZC + (to // 2) * 2 + 1 - to % 2, feat))
+        for k in FAR_8:
+            send(11, f1, rows_of(out_ref, 256 + z * 32, 32), on_z(k))
+        for k in FAR_8 + (0,):
+            send(11, f1, rows_of(out_ref, 256 + z * 32, 32), (on_z(k)[0] - 1, feat))
         own1 = pltpu.make_async_copy(f1, rows_of(out_ref, 256 + z * 32, 32), load_sem.at[10])
         own1.start()
         own0.wait()

time: 42.2 us -> 41.7 us (0.988)
  Pallas kernels: 41.4 us -> 40.9 us
    pallas_call x1, Pallas kernels: 40.7 us -> 40.2 us  [body(): pl.pallas_call(kernel, out_shape=pltpu.VMEM((512, 128), BF16), in_specs=[...]
where the time goes in v7:
time: 41.7 us; the launch traced here: 41.6 us
  Pallas kernels  40.9 us (98%)
  between operations  0.64 us (2%)
    pallas_call x1, Pallas kernels, body(): pl.pallas_call(kernel, out_shape=pltpu.VMEM((512, 128), BF16), in_specs=[...  40.2 us

profile of v7, /device:TPU:1, one launch (start us, length us, event | category | flops | bytes accessed | tf_op | source)
XLA Modules:
  0.0 41.6 jit_solution(15666843984403577330)
XLA Ops:
  0.6 40.2 %sage_backward.1.sums = bf16[512,128]{1,0:T(8,128)(2,1)S(1)} custom-call(bf16[192,256]{1,0:T(8,128)(2,1)} %bitcast.6, bf16[256,256]{1,0:T(8,128)(2,1)} %pa_hbm.1, bf16[64,256]{1,0:T(8,128)(2,1)} %bitcast.7, bf16[64,256]{1,0:T(8,128)(2,1)} %bitcast.8, s32[2,6,128,128]{3,2,1,0:T(8,128)} %adj_hbm.1, s32[2,6]{1,0:T(2,128)} %cols_hbm.1, s32[2]{0:T(128)} %live_hbm.1, ...), custom_call_target="tpu_custom_call" | custom-call | tf_op jit(solution)/shard_map/sage_backward/pallas_call | solution.py:331
  40.9 0.7 %widen.1 = (f32[192,256]{1,0:T(8,128)}, f32[64,256]{1,0:T(8,128)}) custom-call(bf16[512,128]{1,0:T(8,128)(2,1)S(1)} %sage_backward.1.sums), custom_call_target="tpu_custom_call" | custom-call | tf_op jit(solution)/shard_map/widen/pallas_call | solution.py:366

commit v8 on v7

--- a/solution.py
+++ b/solution.py
@@ -176,9 +176,9 @@
     s1[...] = dot_nt(perm, jnp.concatenate([halo_part, halo_part], axis=0)).astype(BF16)
 
     pl.semaphore_wait(barrier, partners)
+    scatter_zc(2, s1, r1, 16)
     for k in FAR_8:
         pl.semaphore_signal(ready_sem, inc=1, device_id=(dom_y(k), feat), device_id_type=MESH)
-    scatter_zc(2, s1, r1, 16)
     scatter_y(0, s0, r0, 32)
     ld_wt.wait()
     for k in FAR_4:

time: 41.7 us -> 42.1 us (level)
  no operation moved by 1% of the time
where the time goes in v8:
time: 42.1 us; the launch traced here: 41.9 us
  Pallas kernels  41.3 us (98%)
  between operations  0.64 us (2%)
    pallas_call x1, Pallas kernels, body(): pl.pallas_call(kernel, out_shape=pltpu.VMEM((512, 128), BF16), in_specs=[...  40.6 us

profile of v8, /device:TPU:1, one launch (start us, length us, event | category | flops | bytes accessed | tf_op | source)
XLA Modules:
  0.0 41.9 jit_solution(9289165264620038794)
XLA Ops:
  0.6 40.6 %sage_backward.1.sums = bf16[512,128]{1,0:T(8,128)(2,1)S(1)} custom-call(bf16[192,256]{1,0:T(8,128)(2,1)} %bitcast.6, bf16[256,256]{1,0:T(8,128)(2,1)} %pa_hbm.1, bf16[64,256]{1,0:T(8,128)(2,1)} %bitcast.7, bf16[64,256]{1,0:T(8,128)(2,1)} %bitcast.8, s32[2,6,128,128]{3,2,1,0:T(8,128)} %adj_hbm.1, s32[2,6]{1,0:T(2,128)} %cols_hbm.1, s32[2]{0:T(128)} %live_hbm.1, ...), custom_call_target="tpu_custom_call" | custom-call | tf_op jit(solution)/shard_map/sage_backward/pallas_call | solution.py:331
  41.2 0.7 %widen.1 = (f32[192,256]{1,0:T(8,128)}, f32[64,256]{1,0:T(8,128)}) custom-call(bf16[512,128]{1,0:T(8,128)(2,1)S(1)} %sage_backward.1.sums), custom_call_target="tpu_custom_call" | custom-call | tf_op jit(solution)/shard_map/widen/pallas_call | solution.py:366
